TPU v7x, 256 devices: a whole 4x4x8 slice. The times are simulated.
256 devices in a mesh: tm: 16 (over y, x), space: 16 (over z, core).
Axes of the slice: x: 4, y: 4, z: 8, core: 2. Of those that a mesh axis runs over, the one named last changes fastest.
Arguments:
- iterate: float32 [16, 16, 256, 1024], P('tm', None, 'space'), may hold values from -1.2 to 1.2
- fine_prev: float32 [16, 16, 256, 1024], P('tm', None, 'space'), may hold values from -1.2 to 1.2
- mobility: float32 [16, 256, 1024], P(None, 'space'), may hold values from 0.5 to 4
- pending: int32 [16], replicated, may hold values 0 or 1
Outputs:
- slice_ends: float32 [16, 16, 256, 1024], P('tm', None, 'space')
All inputs are finite; a program needn't handle non-finite values.
Results may differ from a plain program's by a relative error of at most 0.0003.
Values sent between devices are 32-bit elements; how exact they have to be, the bound alone decides.
No kernel may reach another device: no remote copies, remote signals or barrier semaphores. Data moves between devices by JAX's collectives and lax.ppermute only.
A program may use at most 256 MiB of HBM per device.

v0:
```python
import jax
import jax.numpy as jnp
from jax import lax
from jax.sharding import PartitionSpec as P

FINE_STEPS = 2


DIFFUSE = 0.15
REACTION = 0.1


def extended(cells, sides, width):
    for axis, dim in sides:
        count = lax.axis_size(axis)
        ends = count - 1
        head = lax.slice_in_dim(cells, 0, width, axis=dim)
        tail = lax.slice_in_dim(cells, cells.shape[dim] - width, cells.shape[dim], axis=dim)
        cells = jnp.concatenate(
            [
                lax.ppermute(tail, axis, [(i, (i + 1) % count) for i in range(ends)]),
                cells,
                lax.ppermute(head, axis, [((i + 1) % count, i) for i in range(ends)]),
            ],
            axis=dim,
        )
    return cells


def from_behind(block, axis, distance):
    devices = range(lax.axis_size(axis))
    route = [(i - distance, i) for i in devices if i - distance in devices]
    return lax.ppermute(block, axis, route)


def update(padded, mobility_rows):
    center = padded[:, 1:-1, :]
    framed = jnp.pad(padded, ((1, 1), (0, 0), (1, 1)))
    laplace = (
        framed[2:, 1:-1, 1:-1]
        + framed[:-2, 1:-1, 1:-1]
        + (framed[1:-1, 2:, 1:-1] + framed[1:-1, :-2, 1:-1])
        + (framed[1:-1, 1:-1, 2:] + framed[1:-1, 1:-1, :-2])
        - 6.0 * center
    )
    return (
        center + DIFFUSE * laplace + REACTION * mobility_rows * (center - center * center * center)
    )


def coarse_update(padded, coarse_mobility):
    center = padded[:, 1:-1, :]
    framed = jnp.pad(padded, ((1, 1), (0, 0), (1, 1)))
    along_x = framed[1:-1, 2:, 1:-1] + framed[1:-1, :-2, 1:-1] - 2.0 * center
    along_y = framed[1:-1, 1:-1, 2:] + framed[1:-1, 1:-1, :-2] - 2.0 * center
    along_z = framed[2:, 1:-1, 1:-1] + framed[:-2, 1:-1, 1:-1] - 2.0 * center
    laplace = 0.25 * along_x + 0.25 * along_y + along_z
    rate = 2.0 * REACTION * coarse_mobility
    return (
        center
        + 2.0 * DIFFUSE * laplace
        + rate * (center - center * center * center) / (1.0 + rate * center * center)
    )


def restrict(field):
    layer_count, row_count, col_count = field.shape
    blocks = field.reshape(layer_count, row_count // 2, 2, col_count // 2, 2)
    return 0.25 * jnp.sum(blocks, axis=(2, 4))


def prolong(coarse_field):
    return jnp.repeat(jnp.repeat(coarse_field, 2, axis=1), 2, axis=2)


def coarse_advance(coarse_field, coarse_mobility):
    padded = extended(coarse_field, (("space", 1),), 1)
    return coarse_update(padded, coarse_mobility)


def local(iterate, fine_prev, mobility, pending):
    slice_index = lax.axis_index("tm")
    slice_count = lax.axis_size("tm")
    flagged = jnp.sum(
        jnp.where(jnp.arange(pending.shape[0], dtype=jnp.int32) == slice_index, pending, 0)
    )
    start_state = iterate[0]
    fine_state = start_state
    for _ in range(FINE_STEPS):
        padded = extended(fine_state, (("space", 1),), 1)
        fine_state = update(padded, mobility)
    fine_state = jnp.where(flagged > 0, fine_state, fine_prev[0])
    coarse_mobility = restrict(mobility)
    coarse_start = restrict(start_state)
    fine_coarse = restrict(fine_state)

    def advance(field):
        return coarse_advance(field, coarse_mobility)

    base_start, base_fine = (coarse_start, fine_coarse)
    coarse_old = advance(base_start)
    jump_term = base_fine - coarse_old

    def advance_link(turn_index, coarse_now):
        stepped = advance(coarse_now)
        arrived = from_behind(stepped + jump_term, "tm", 1)
        return jnp.where(slice_index == turn_index + 1, arrived, coarse_now)

    coarse_now = lax.fori_loop(0, slice_count - 1, advance_link, base_start)
    advanced = advance(coarse_now)
    correction = advanced - coarse_old
    return (fine_state + prolong(correction))[None]


def solution(mesh):
    placed = (
        P("tm", None, "space", None),
        P("tm", None, "space", None),
        P(None, "space", None),
        P(),
    )
    return jax.shard_map(
        local, mesh=mesh, in_specs=placed, out_specs=P("tm", None, "space", None), check_vma=False
    )
```

profile of v0, /device:TPU:105, one launch (start us, length us, event | category | flops | bytes accessed | tf_op | source)
XLA Modules:
  0.0 412.7 jit_solution(12759326281225974259)
XLA Ops:
  3.9 4.7 %collective-permute-start.3 = (f32[16,1,1024]{2,0,1:T(8,128)S(1)}, f32[16,1,1024]{2,0,1:T(8,128)S(1)}, u32[]{:S(2)}, u32[]{:S(2)}) collective-permute-start(f32[16,1,1024]{2,0,1:T(8,128)S(1)} %copy.208), channel_id=1, source_target_pairs={{0,1},{1,2},{2,3},{3,4},{4,5},{5,6},{6,7},{7,8},{8,9},{9,10},{10,1... | collective-permute-start | bytes 196616 | tf_op jit(solution)/shard_map/ppermute | solution.py:21
  8.6 5.9 %copy.220 = f32[1,16,16,1024]{1,3,2,0:T(8,128)} copy(f32[1,16,16,1024]{3,2,1,0:T(8,128)} %param.6) | data formatting | bytes 2097152 | tf_op args[0]
  14.5 10.7 %reduce_sum.37 = f32[16,8,512]{0,2,1:T(8,128)} reduce(f32[16,8,2,512,2]{0,4,3,2,1:T(2,128)} %bitcast.12, f32[]{:T(128)} %constant.89.clone.1), dimensions={2,4}, to_apply=%region_1.2 | reduce | flops 196608 | bytes 1310724 | tf_op jit(solution)/shard_map/reduce_sum | solution.py:69
  32.0 4.6 %copy.222 = f32[16,16,1024]{0,2,1:T(8,128)} copy(f32[16,16,1024]{2,1,0:T(8,128)S(1)} %copy-done.1) | data formatting | bytes 2097152 | tf_op args[2]
  36.6 10.7 %reduce_sum.38 = f32[16,8,512]{0,2,1:T(8,128)} reduce(f32[16,8,2,512,2]{0,4,3,2,1:T(2,128)} %bitcast.13, f32[]{:T(128)} %constant.89.clone.1), dimensions={2,4}, to_apply=%region_2.3 | reduce | flops 196608 | bytes 1310724 | tf_op jit(solution)/shard_map/reduce_sum | solution.py:69
  56.1 5.0 %collective-permute-start.5 = (f32[16,1,1024]{2,0,1:T(8,128)S(1)}, f32[16,1,1024]{2,0,1:T(8,128)S(1)}, u32[]{:S(2)}, u32[]{:S(2)}) collective-permute-start(f32[16,1,1024]{2,0,1:T(8,128)S(1)} %copy.214), channel_id=1, source_target_pairs={{0,1},{1,2},{2,3},{3,4},{4,5},{5,6},{6,7},{7,8},{8,9},{9,10},{10,1... | collective-permute-start | bytes 196616 | tf_op jit(solution)/shard_map/ppermute | solution.py:21
  64.8 4.6 %copy.224 = f32[16,16,1024]{0,2,1:T(8,128)} copy(f32[16,16,1024]{2,1,0:T(8,128)S(1)} %fusion.23) | data formatting | bytes 2097152 | tf_op jit(solution)/shard_map/jit(_where)/select_n | solution.py:92
  69.4 9.6 %reduce_sum.39 = f32[16,8,512]{0,2,1:T(8,128)S(1)} reduce(f32[16,8,2,512,2]{0,4,3,2,1:T(2,128)} %bitcast.11, f32[]{:T(128)} %constant.89.clone.1), dimensions={2,4}, to_apply=%region_3.4 | reduce | flops 196608 | bytes 1310724 | tf_op jit(solution)/shard_map/reduce_sum | solution.py:69
  83.0 300.6 %while.15 = (s32[]{:T(128)}, f32[16,8,512]{2,1,0:T(8,128)S(1)}, s32[]{:T(128)}, f32[16,8,512]{2,1,0:T(8,128)S(1)}, f32[16,8,512]{2,1,0:T(8,128)S(1)}, /*index=5*/s32[]{:T(128)}) while((s32[]{:T(128)}, f32[16,8,512]{2,1,0:T(8,128)S(1)}, s32[]{:T(128)}, f32[16,8,512]{2,1,0:T(8,128)S(1)}, f32[16,8,512]{2,1,0:T(8,128)S(1)}, ...), condition=%wide.region_5.6_spmd, body=%wide.region_4.5_spmd.sunk | while | flops 3091739 | bytes 5088871 | solution.py:109
  85.0 5.2 %collective-permute-start.1 = (f32[16,1,512]{2,1,0:T(1,128)S(1)}, f32[16,1,512]{2,1,0:T(1,128)S(1)}, u32[]{:S(2)}, u32[]{:S(2)}) collective-permute-start(f32[16,1,512]{2,1,0:T(1,128)S(1)} %get-tuple-element.212), channel_id=1, source_target_pairs={{0,1},{1,2},{2,3},{3,4},{4,5},{5,6},{6,7},{7,8},{8,9},{9,10},{10,1... | collective-permute-start | bytes 98312 | tf_op jit(solution)/shard_map/while/body/eval_jaxpr/ppermute | solution.py:21
  92.0 3.1 collective-permute-start.2
  95.2 7.5 %collective-permute-done.2 = f32[16,8,512]{2,1,0:T(8,128)S(1)} collective-permute-done((f32[16,8,512]{2,1,0:T(8,128)S(1)}, f32[16,8,512]{2,1,0:T(8,128)S(1)}, u32[]{:S(2)}, u32[]{:S(2)}) %collective-permute-start.2) | collective-permute-done | bytes 262176 | tf_op jit(solution)/shard_map/while/body/eval_jaxpr/ppermute | solution.py:33
  104.7 5.1 %collective-permute-start.1 = (f32[16,1,512]{2,1,0:T(1,128)S(1)}, f32[16,1,512]{2,1,0:T(1,128)S(1)}, u32[]{:S(2)}, u32[]{:S(2)}) collective-permute-start(f32[16,1,512]{2,1,0:T(1,128)S(1)} %get-tuple-element.212), channel_id=1, source_target_pairs={{0,1},{1,2},{2,3},{3,4},{4,5},{5,6},{6,7},{7,8},{8,9},{9,10},{10,1... | collective-permute-start | bytes 98312 | tf_op jit(solution)/shard_map/while/body/eval_jaxpr/ppermute | solution.py:21
  113.7 8.9 %collective-permute-done.2 = f32[16,8,512]{2,1,0:T(8,128)S(1)} collective-permute-done((f32[16,8,512]{2,1,0:T(8,128)S(1)}, f32[16,8,512]{2,1,0:T(8,128)S(1)}, u32[]{:S(2)}, u32[]{:S(2)}) %collective-permute-start.2) | collective-permute-done | bytes 262176 | tf_op jit(solution)/shard_map/while/body/eval_jaxpr/ppermute | solution.py:33
  124.6 5.0 %collective-permute-start.1 = (f32[16,1,512]{2,1,0:T(1,128)S(1)}, f32[16,1,512]{2,1,0:T(1,128)S(1)}, u32[]{:S(2)}, u32[]{:S(2)}) collective-permute-start(f32[16,1,512]{2,1,0:T(1,128)S(1)} %get-tuple-element.212), channel_id=1, source_target_pairs={{0,1},{1,2},{2,3},{3,4},{4,5},{5,6},{6,7},{7,8},{8,9},{9,10},{10,1... | collective-permute-start | bytes 98312 | tf_op jit(solution)/shard_map/while/body/eval_jaxpr/ppermute | solution.py:21
  133.3 9.3 %collective-permute-done.2 = f32[16,8,512]{2,1,0:T(8,128)S(1)} collective-permute-done((f32[16,8,512]{2,1,0:T(8,128)S(1)}, f32[16,8,512]{2,1,0:T(8,128)S(1)}, u32[]{:S(2)}, u32[]{:S(2)}) %collective-permute-start.2) | collective-permute-done | bytes 262176 | tf_op jit(solution)/shard_map/while/body/eval_jaxpr/ppermute | solution.py:33
  144.7 4.9 %collective-permute-start.1 = (f32[16,1,512]{2,1,0:T(1,128)S(1)}, f32[16,1,512]{2,1,0:T(1,128)S(1)}, u32[]{:S(2)}, u32[]{:S(2)}) collective-permute-start(f32[16,1,512]{2,1,0:T(1,128)S(1)} %get-tuple-element.212), channel_id=1, source_target_pairs={{0,1},{1,2},{2,3},{3,4},{4,5},{5,6},{6,7},{7,8},{8,9},{9,10},{10,1... | collective-permute-start | bytes 98312 | tf_op jit(solution)/shard_map/while/body/eval_jaxpr/ppermute | solution.py:21
  153.3 9.9 %collective-permute-done.2 = f32[16,8,512]{2,1,0:T(8,128)S(1)} collective-permute-done((f32[16,8,512]{2,1,0:T(8,128)S(1)}, f32[16,8,512]{2,1,0:T(8,128)S(1)}, u32[]{:S(2)}, u32[]{:S(2)}) %collective-permute-start.2) | collective-permute-done | bytes 262176 | tf_op jit(solution)/shard_map/while/body/eval_jaxpr/ppermute | solution.py:33
  165.6 4.5 %collective-permute-start.1 = (f32[16,1,512]{2,1,0:T(1,128)S(1)}, f32[16,1,512]{2,1,0:T(1,128)S(1)}, u32[]{:S(2)}, u32[]{:S(2)}) collective-permute-start(f32[16,1,512]{2,1,0:T(1,128)S(1)} %get-tuple-element.212), channel_id=1, source_target_pairs={{0,1},{1,2},{2,3},{3,4},{4,5},{5,6},{6,7},{7,8},{8,9},{9,10},{10,1... | collective-permute-start | bytes 98312 | tf_op jit(solution)/shard_map/while/body/eval_jaxpr/ppermute | solution.py:21
  173.9 10.2 %collective-permute-done.2 = f32[16,8,512]{2,1,0:T(8,128)S(1)} collective-permute-done((f32[16,8,512]{2,1,0:T(8,128)S(1)}, f32[16,8,512]{2,1,0:T(8,128)S(1)}, u32[]{:S(2)}, u32[]{:S(2)}) %collective-permute-start.2) | collective-permute-done | bytes 262176 | tf_op jit(solution)/shard_map/while/body/eval_jaxpr/ppermute | solution.py:33
  186.7 4.2 %collective-permute-start.1 = (f32[16,1,512]{2,1,0:T(1,128)S(1)}, f32[16,1,512]{2,1,0:T(1,128)S(1)}, u32[]{:S(2)}, u32[]{:S(2)}) collective-permute-start(f32[16,1,512]{2,1,0:T(1,128)S(1)} %get-tuple-element.212), channel_id=1, source_target_pairs={{0,1},{1,2},{2,3},{3,4},{4,5},{5,6},{6,7},{7,8},{8,9},{9,10},{10,1... | collective-permute-start | bytes 98312 | tf_op jit(solution)/shard_map/while/body/eval_jaxpr/ppermute | solution.py:21
  194.7 10.0 %collective-permute-done.2 = f32[16,8,512]{2,1,0:T(8,128)S(1)} collective-permute-done((f32[16,8,512]{2,1,0:T(8,128)S(1)}, f32[16,8,512]{2,1,0:T(8,128)S(1)}, u32[]{:S(2)}, u32[]{:S(2)}) %collective-permute-start.2) | collective-permute-done | bytes 262176 | tf_op jit(solution)/shard_map/while/body/eval_jaxpr/ppermute | solution.py:33
  207.5 4.1 collective-permute-start.1
  215.4 9.8 %collective-permute-done.2 = f32[16,8,512]{2,1,0:T(8,128)S(1)} collective-permute-done((f32[16,8,512]{2,1,0:T(8,128)S(1)}, f32[16,8,512]{2,1,0:T(8,128)S(1)}, u32[]{:S(2)}, u32[]{:S(2)}) %collective-permute-start.2) | collective-permute-done | bytes 262176 | tf_op jit(solution)/shard_map/while/body/eval_jaxpr/ppermute | solution.py:33
  228.2 3.9 collective-permute-start.1
  235.9 9.6 %collective-permute-done.2 = f32[16,8,512]{2,1,0:T(8,128)S(1)} collective-permute-done((f32[16,8,512]{2,1,0:T(8,128)S(1)}, f32[16,8,512]{2,1,0:T(8,128)S(1)}, u32[]{:S(2)}, u32[]{:S(2)}) %collective-permute-start.2) | collective-permute-done | bytes 262176 | tf_op jit(solution)/shard_map/while/body/eval_jaxpr/ppermute | solution.py:33
  248.7 3.7 collective-permute-start.1
  256.2 9.4 %collective-permute-done.2 = f32[16,8,512]{2,1,0:T(8,128)S(1)} collective-permute-done((f32[16,8,512]{2,1,0:T(8,128)S(1)}, f32[16,8,512]{2,1,0:T(8,128)S(1)}, u32[]{:S(2)}, u32[]{:S(2)}) %collective-permute-start.2) | collective-permute-done | bytes 262176 | tf_op jit(solution)/shard_map/while/body/eval_jaxpr/ppermute | solution.py:33
  265.7 3.3 collective-permute-start
  269.0 3.5 collective-permute-start.1
  276.2 9.1 %collective-permute-done.2 = f32[16,8,512]{2,1,0:T(8,128)S(1)} collective-permute-done((f32[16,8,512]{2,1,0:T(8,128)S(1)}, f32[16,8,512]{2,1,0:T(8,128)S(1)}, u32[]{:S(2)}, u32[]{:S(2)}) %collective-permute-start.2) | collective-permute-done | bytes 262176 | tf_op jit(solution)/shard_map/while/body/eval_jaxpr/ppermute | solution.py:33
  285.5 3.6 collective-permute-start
  289.1 3.2 collective-permute-start.1
  296.1 8.8 %collective-permute-done.2 = f32[16,8,512]{2,1,0:T(8,128)S(1)} collective-permute-done((f32[16,8,512]{2,1,0:T(8,128)S(1)}, f32[16,8,512]{2,1,0:T(8,128)S(1)}, u32[]{:S(2)}, u32[]{:S(2)}) %collective-permute-start.2) | collective-permute-done | bytes 262176 | tf_op jit(solution)/shard_map/while/body/eval_jaxpr/ppermute | solution.py:33
  305.0 3.9 collective-permute-start
  308.9 3.1 collective-permute-start.1
  315.8 8.7 %collective-permute-done.2 = f32[16,8,512]{2,1,0:T(8,128)S(1)} collective-permute-done((f32[16,8,512]{2,1,0:T(8,128)S(1)}, f32[16,8,512]{2,1,0:T(8,128)S(1)}, u32[]{:S(2)}, u32[]{:S(2)}) %collective-permute-start.2) | collective-permute-done | bytes 262176 | tf_op jit(solution)/shard_map/while/body/eval_jaxpr/ppermute | solution.py:33
  324.6 4.0 collective-permute-start
  335.4 8.7 %collective-permute-done.2 = f32[16,8,512]{2,1,0:T(8,128)S(1)} collective-permute-done((f32[16,8,512]{2,1,0:T(8,128)S(1)}, f32[16,8,512]{2,1,0:T(8,128)S(1)}, u32[]{:S(2)}, u32[]{:S(2)}) %collective-permute-start.2) | collective-permute-done | bytes 262176 | tf_op jit(solution)/shard_map/while/body/eval_jaxpr/ppermute | solution.py:33
  344.3 4.0 collective-permute-start
  355.1 8.7 %collective-permute-done.2 = f32[16,8,512]{2,1,0:T(8,128)S(1)} collective-permute-done((f32[16,8,512]{2,1,0:T(8,128)S(1)}, f32[16,8,512]{2,1,0:T(8,128)S(1)}, u32[]{:S(2)}, u32[]{:S(2)}) %collective-permute-start.2) | collective-permute-done | bytes 262176 | tf_op jit(solution)/shard_map/while/body/eval_jaxpr/ppermute | solution.py:33
  364.0 4.0 collective-permute-start
  374.8 8.7 %collective-permute-done.2 = f32[16,8,512]{2,1,0:T(8,128)S(1)} collective-permute-done((f32[16,8,512]{2,1,0:T(8,128)S(1)}, f32[16,8,512]{2,1,0:T(8,128)S(1)}, u32[]{:S(2)}, u32[]{:S(2)}) %collective-permute-start.2) | collective-permute-done | bytes 262176 | tf_op jit(solution)/shard_map/while/body/eval_jaxpr/ppermute | solution.py:33
  383.8 5.1 %collective-permute-start.10 = (f32[16,1,512]{2,0,1:T(8,128)S(1)}, f32[16,1,512]{2,0,1:T(8,128)S(1)}, u32[]{:S(2)}, u32[]{:S(2)}) collective-permute-start(f32[16,1,512]{2,0,1:T(8,128)S(1)} %get-tuple-element.173), channel_id=1, source_target_pairs={{0,1},{1,2},{2,3},{3,4},{4,5},{5,6},{6,7},{7,8},{8,9},{9,10},{10,1... | collective-permute-start | bytes 98312 | tf_op jit(solution)/shard_map/ppermute | solution.py:21
  390.9 4.5 %collective-permute-done.9 = f32[16,1,512]{2,0,1:T(8,128)S(1)} collective-permute-done((f32[16,1,512]{2,0,1:T(8,128)S(1)}, f32[16,1,512]{2,0,1:T(8,128)S(1)}, u32[]{:S(2)}, u32[]{:S(2)}) %collective-permute-start.9) | collective-permute-done | bytes 32800 | tf_op jit(solution)/shard_map/ppermute | solution.py:23
  396.5 3.8 copy.237
  400.3 6.1 %broadcast_in_dim.15 = f32[16,16,512,2]{1,0,3,2:T(8,128)} broadcast(f32[16,16,512]{1,0,2:T(8,128)} %copy.237), dimensions={0,1,2} | broadcast | bytes 1572864 | tf_op jit(solution)/shard_map/broadcast_in_dim | solution.py:73
  406.4 5.1 %copy.238 = f32[16,16,1024]{2,1,0:T(8,128)S(1)} copy(f32[16,16,1024]{1,0,2:T(8,128)} %bitcast.10) | data formatting | bytes 2097152 | tf_op jit(solution)/shard_map/reshape | solution.py:73
  (171 shorter events, 116.4 us)
Async XLA Ops:
  1.3 50.3 %collective-permute-start.4 = (f32[16,1,1024]{2,0,1:T(8,128)S(1)}, f32[16,1,1024]{2,0,1:T(8,128)S(1)}, u32[]{:S(2)}, u32[]{:S(2)}) collective-permute-start(f32[16,1,1024]{2,0,1:T(8,128)S(1)} %copy.209), channel_id=1, source_target_pairs={{1,0},{2,1},{3,2},{4,3},{5,4},{6,5},{7,6},{8,7},{9,8},{10,9},{11,1... | collective-permute-start | bytes 196616 | tf_op jit(solution)/shard_map/ppermute | solution.py:23
  3.9 47.8 %collective-permute-start.3 = (f32[16,1,1024]{2,0,1:T(8,128)S(1)}, f32[16,1,1024]{2,0,1:T(8,128)S(1)}, u32[]{:S(2)}, u32[]{:S(2)}) collective-permute-start(f32[16,1,1024]{2,0,1:T(8,128)S(1)} %copy.208), channel_id=1, source_target_pairs={{0,1},{1,2},{2,3},{3,4},{4,5},{5,6},{6,7},{7,8},{8,9},{9,10},{10,1... | collective-permute-start | bytes 196616 | tf_op jit(solution)/shard_map/ppermute | solution.py:21
  27.6 33.5 %collective-permute-start.8 = (f32[16,1,512]{2,1,0:T(1,128)S(1)}, f32[16,1,512]{2,1,0:T(1,128)S(1)}, u32[]{:S(2)}, u32[]{:S(2)}) collective-permute-start(f32[16,1,512]{2,1,0:T(1,128)S(1)} %get-tuple-element.176), channel_id=1, source_target_pairs={{0,1},{1,2},{2,3},{3,4},{4,5},{5,6},{6,7},{7,8},{8,9},{9,10},{10,1... | collective-permute-start | bytes 98312 | tf_op jit(solution)/shard_map/ppermute | solution.py:21
  30.1 31.1 %collective-permute-start.7 = (f32[16,1,512]{2,1,0:T(1,128)S(1)}, f32[16,1,512]{2,1,0:T(1,128)S(1)}, u32[]{:S(2)}, u32[]{:S(2)}) collective-permute-start(f32[16,1,512]{2,1,0:T(1,128)S(1)} %get-tuple-element.177), channel_id=1, source_target_pairs={{1,0},{2,1},{3,2},{4,3},{5,4},{6,5},{7,6},{8,7},{9,8},{10,9},{11,1... | collective-permute-start | bytes 98312 | tf_op jit(solution)/shard_map/ppermute | solution.py:23
  54.1 8.4 %collective-permute-start.6 = (f32[16,1,1024]{2,0,1:T(8,128)S(1)}, f32[16,1,1024]{2,0,1:T(8,128)S(1)}, u32[]{:S(2)}, u32[]{:S(2)}) collective-permute-start(f32[16,1,1024]{2,0,1:T(8,128)S(1)} %copy.215), channel_id=1, source_target_pairs={{1,0},{2,1},{3,2},{4,3},{5,4},{6,5},{7,6},{8,7},{9,8},{10,9},{11,1... | collective-permute-start | bytes 196616 | tf_op jit(solution)/shard_map/ppermute | solution.py:23
  56.1 6.4 %collective-permute-start.5 = (f32[16,1,1024]{2,0,1:T(8,128)S(1)}, f32[16,1,1024]{2,0,1:T(8,128)S(1)}, u32[]{:S(2)}, u32[]{:S(2)}) collective-permute-start(f32[16,1,1024]{2,0,1:T(8,128)S(1)} %copy.214), channel_id=1, source_target_pairs={{0,1},{1,2},{2,3},{3,4},{4,5},{5,6},{6,7},{7,8},{8,9},{9,10},{10,1... | collective-permute-start | bytes 196616 | tf_op jit(solution)/shard_map/ppermute | solution.py:21
  83.1 7.1 %collective-permute-start = (f32[16,1,512]{2,1,0:T(1,128)S(1)}, f32[16,1,512]{2,1,0:T(1,128)S(1)}, u32[]{:S(2)}, u32[]{:S(2)}) collective-permute-start(f32[16,1,512]{2,1,0:T(1,128)S(1)} %get-tuple-element.211), channel_id=1, source_target_pairs={{1,0},{2,1},{3,2},{4,3},{5,4},{6,5},{7,6},{8,7},{9,8},{10,9},{11,1... | collective-permute-start | bytes 98312 | tf_op jit(solution)/shard_map/while/body/eval_jaxpr/ppermute | solution.py:23
  85.0 6.2 %collective-permute-start.1 = (f32[16,1,512]{2,1,0:T(1,128)S(1)}, f32[16,1,512]{2,1,0:T(1,128)S(1)}, u32[]{:S(2)}, u32[]{:S(2)}) collective-permute-start(f32[16,1,512]{2,1,0:T(1,128)S(1)} %get-tuple-element.212), channel_id=1, source_target_pairs={{0,1},{1,2},{2,3},{3,4},{4,5},{5,6},{6,7},{7,8},{8,9},{9,10},{10,1... | collective-permute-start | bytes 98312 | tf_op jit(solution)/shard_map/while/body/eval_jaxpr/ppermute | solution.py:21
  92.0 10.7 %collective-permute-start.2 = (f32[16,8,512]{2,1,0:T(8,128)S(1)}, f32[16,8,512]{2,1,0:T(8,128)S(1)}, u32[]{:S(2)}, u32[]{:S(2)}) collective-permute-start(f32[16,8,512]{2,1,0:T(8,128)S(1)} %fusion.76), channel_id=1, source_target_pairs={{0,16},{16,32},{32,48},{48,64},{64,80},{80,96},{96,112},{112,128},... | collective-permute-start | bytes 786440 | tf_op jit(solution)/shard_map/while/body/eval_jaxpr/ppermute | solution.py:33
  102.8 7.1 %collective-permute-start = (f32[16,1,512]{2,1,0:T(1,128)S(1)}, f32[16,1,512]{2,1,0:T(1,128)S(1)}, u32[]{:S(2)}, u32[]{:S(2)}) collective-permute-start(f32[16,1,512]{2,1,0:T(1,128)S(1)} %get-tuple-element.211), channel_id=1, source_target_pairs={{1,0},{2,1},{3,2},{4,3},{5,4},{6,5},{7,6},{8,7},{9,8},{10,9},{11,1... | collective-permute-start | bytes 98312 | tf_op jit(solution)/shard_map/while/body/eval_jaxpr/ppermute | solution.py:23
  104.7 6.2 %collective-permute-start.1 = (f32[16,1,512]{2,1,0:T(1,128)S(1)}, f32[16,1,512]{2,1,0:T(1,128)S(1)}, u32[]{:S(2)}, u32[]{:S(2)}) collective-permute-start(f32[16,1,512]{2,1,0:T(1,128)S(1)} %get-tuple-element.212), channel_id=1, source_target_pairs={{0,1},{1,2},{2,3},{3,4},{4,5},{5,6},{6,7},{7,8},{8,9},{9,10},{10,1... | collective-permute-start | bytes 98312 | tf_op jit(solution)/shard_map/while/body/eval_jaxpr/ppermute | solution.py:21
  111.7 10.8 %collective-permute-start.2 = (f32[16,8,512]{2,1,0:T(8,128)S(1)}, f32[16,8,512]{2,1,0:T(8,128)S(1)}, u32[]{:S(2)}, u32[]{:S(2)}) collective-permute-start(f32[16,8,512]{2,1,0:T(8,128)S(1)} %fusion.76), channel_id=1, source_target_pairs={{0,16},{16,32},{32,48},{48,64},{64,80},{80,96},{96,112},{112,128},... | collective-permute-start | bytes 786440 | tf_op jit(solution)/shard_map/while/body/eval_jaxpr/ppermute | solution.py:33
  122.7 6.9 %collective-permute-start = (f32[16,1,512]{2,1,0:T(1,128)S(1)}, f32[16,1,512]{2,1,0:T(1,128)S(1)}, u32[]{:S(2)}, u32[]{:S(2)}) collective-permute-start(f32[16,1,512]{2,1,0:T(1,128)S(1)} %get-tuple-element.211), channel_id=1, source_target_pairs={{1,0},{2,1},{3,2},{4,3},{5,4},{6,5},{7,6},{8,7},{9,8},{10,9},{11,1... | collective-permute-start | bytes 98312 | tf_op jit(solution)/shard_map/while/body/eval_jaxpr/ppermute | solution.py:23
  124.6 6.0 %collective-permute-start.1 = (f32[16,1,512]{2,1,0:T(1,128)S(1)}, f32[16,1,512]{2,1,0:T(1,128)S(1)}, u32[]{:S(2)}, u32[]{:S(2)}) collective-permute-start(f32[16,1,512]{2,1,0:T(1,128)S(1)} %get-tuple-element.212), channel_id=1, source_target_pairs={{0,1},{1,2},{2,3},{3,4},{4,5},{5,6},{6,7},{7,8},{8,9},{9,10},{10,1... | collective-permute-start | bytes 98312 | tf_op jit(solution)/shard_map/while/body/eval_jaxpr/ppermute | solution.py:21
  131.4 11.2 %collective-permute-start.2 = (f32[16,8,512]{2,1,0:T(8,128)S(1)}, f32[16,8,512]{2,1,0:T(8,128)S(1)}, u32[]{:S(2)}, u32[]{:S(2)}) collective-permute-start(f32[16,8,512]{2,1,0:T(8,128)S(1)} %fusion.76), channel_id=1, source_target_pairs={{0,16},{16,32},{32,48},{48,64},{64,80},{80,96},{96,112},{112,128},... | collective-permute-start | bytes 786440 | tf_op jit(solution)/shard_map/while/body/eval_jaxpr/ppermute | solution.py:33
  142.8 6.8 %collective-permute-start = (f32[16,1,512]{2,1,0:T(1,128)S(1)}, f32[16,1,512]{2,1,0:T(1,128)S(1)}, u32[]{:S(2)}, u32[]{:S(2)}) collective-permute-start(f32[16,1,512]{2,1,0:T(1,128)S(1)} %get-tuple-element.211), channel_id=1, source_target_pairs={{1,0},{2,1},{3,2},{4,3},{5,4},{6,5},{7,6},{8,7},{9,8},{10,9},{11,1... | collective-permute-start | bytes 98312 | tf_op jit(solution)/shard_map/while/body/eval_jaxpr/ppermute | solution.py:23
  144.7 5.9 %collective-permute-start.1 = (f32[16,1,512]{2,1,0:T(1,128)S(1)}, f32[16,1,512]{2,1,0:T(1,128)S(1)}, u32[]{:S(2)}, u32[]{:S(2)}) collective-permute-start(f32[16,1,512]{2,1,0:T(1,128)S(1)} %get-tuple-element.212), channel_id=1, source_target_pairs={{0,1},{1,2},{2,3},{3,4},{4,5},{5,6},{6,7},{7,8},{8,9},{9,10},{10,1... | collective-permute-start | bytes 98312 | tf_op jit(solution)/shard_map/while/body/eval_jaxpr/ppermute | solution.py:21
  151.4 11.8 %collective-permute-start.2 = (f32[16,8,512]{2,1,0:T(8,128)S(1)}, f32[16,8,512]{2,1,0:T(8,128)S(1)}, u32[]{:S(2)}, u32[]{:S(2)}) collective-permute-start(f32[16,8,512]{2,1,0:T(8,128)S(1)} %fusion.76), channel_id=1, source_target_pairs={{0,16},{16,32},{32,48},{48,64},{64,80},{80,96},{96,112},{112,128},... | collective-permute-start | bytes 786440 | tf_op jit(solution)/shard_map/while/body/eval_jaxpr/ppermute | solution.py:33
  163.3 6.8 %collective-permute-start = (f32[16,1,512]{2,1,0:T(1,128)S(1)}, f32[16,1,512]{2,1,0:T(1,128)S(1)}, u32[]{:S(2)}, u32[]{:S(2)}) collective-permute-start(f32[16,1,512]{2,1,0:T(1,128)S(1)} %get-tuple-element.211), channel_id=1, source_target_pairs={{1,0},{2,1},{3,2},{4,3},{5,4},{6,5},{7,6},{8,7},{9,8},{10,9},{11,1... | collective-permute-start | bytes 98312 | tf_op jit(solution)/shard_map/while/body/eval_jaxpr/ppermute | solution.py:23
  165.6 5.5 %collective-permute-start.1 = (f32[16,1,512]{2,1,0:T(1,128)S(1)}, f32[16,1,512]{2,1,0:T(1,128)S(1)}, u32[]{:S(2)}, u32[]{:S(2)}) collective-permute-start(f32[16,1,512]{2,1,0:T(1,128)S(1)} %get-tuple-element.212), channel_id=1, source_target_pairs={{0,1},{1,2},{2,3},{3,4},{4,5},{5,6},{6,7},{7,8},{8,9},{9,10},{10,1... | collective-permute-start | bytes 98312 | tf_op jit(solution)/shard_map/while/body/eval_jaxpr/ppermute | solution.py:21
  171.9 12.1 %collective-permute-start.2 = (f32[16,8,512]{2,1,0:T(8,128)S(1)}, f32[16,8,512]{2,1,0:T(8,128)S(1)}, u32[]{:S(2)}, u32[]{:S(2)}) collective-permute-start(f32[16,8,512]{2,1,0:T(8,128)S(1)} %fusion.76), channel_id=1, source_target_pairs={{0,16},{16,32},{32,48},{48,64},{64,80},{80,96},{96,112},{112,128},... | collective-permute-start | bytes 786440 | tf_op jit(solution)/shard_map/while/body/eval_jaxpr/ppermute | solution.py:33
  184.2 6.8 %collective-permute-start = (f32[16,1,512]{2,1,0:T(1,128)S(1)}, f32[16,1,512]{2,1,0:T(1,128)S(1)}, u32[]{:S(2)}, u32[]{:S(2)}) collective-permute-start(f32[16,1,512]{2,1,0:T(1,128)S(1)} %get-tuple-element.211), channel_id=1, source_target_pairs={{1,0},{2,1},{3,2},{4,3},{5,4},{6,5},{7,6},{8,7},{9,8},{10,9},{11,1... | collective-permute-start | bytes 98312 | tf_op jit(solution)/shard_map/while/body/eval_jaxpr/ppermute | solution.py:23
  186.7 5.2 %collective-permute-start.1 = (f32[16,1,512]{2,1,0:T(1,128)S(1)}, f32[16,1,512]{2,1,0:T(1,128)S(1)}, u32[]{:S(2)}, u32[]{:S(2)}) collective-permute-start(f32[16,1,512]{2,1,0:T(1,128)S(1)} %get-tuple-element.212), channel_id=1, source_target_pairs={{0,1},{1,2},{2,3},{3,4},{4,5},{5,6},{6,7},{7,8},{8,9},{9,10},{10,1... | collective-permute-start | bytes 98312 | tf_op jit(solution)/shard_map/while/body/eval_jaxpr/ppermute | solution.py:21
  192.8 11.9 %collective-permute-start.2 = (f32[16,8,512]{2,1,0:T(8,128)S(1)}, f32[16,8,512]{2,1,0:T(8,128)S(1)}, u32[]{:S(2)}, u32[]{:S(2)}) collective-permute-start(f32[16,8,512]{2,1,0:T(8,128)S(1)} %fusion.76), channel_id=1, source_target_pairs={{0,16},{16,32},{32,48},{48,64},{64,80},{80,96},{96,112},{112,128},... | collective-permute-start | bytes 786440 | tf_op jit(solution)/shard_map/while/body/eval_jaxpr/ppermute | solution.py:33
  204.8 6.8 %collective-permute-start = (f32[16,1,512]{2,1,0:T(1,128)S(1)}, f32[16,1,512]{2,1,0:T(1,128)S(1)}, u32[]{:S(2)}, u32[]{:S(2)}) collective-permute-start(f32[16,1,512]{2,1,0:T(1,128)S(1)} %get-tuple-element.211), channel_id=1, source_target_pairs={{1,0},{2,1},{3,2},{4,3},{5,4},{6,5},{7,6},{8,7},{9,8},{10,9},{11,1... | collective-permute-start | bytes 98312 | tf_op jit(solution)/shard_map/while/body/eval_jaxpr/ppermute | solution.py:23
  207.5 5.1 %collective-permute-start.1 = (f32[16,1,512]{2,1,0:T(1,128)S(1)}, f32[16,1,512]{2,1,0:T(1,128)S(1)}, u32[]{:S(2)}, u32[]{:S(2)}) collective-permute-start(f32[16,1,512]{2,1,0:T(1,128)S(1)} %get-tuple-element.212), channel_id=1, source_target_pairs={{0,1},{1,2},{2,3},{3,4},{4,5},{5,6},{6,7},{7,8},{8,9},{9,10},{10,1... | collective-permute-start | bytes 98312 | tf_op jit(solution)/shard_map/while/body/eval_jaxpr/ppermute | solution.py:21
  213.4 11.8 %collective-permute-start.2 = (f32[16,8,512]{2,1,0:T(8,128)S(1)}, f32[16,8,512]{2,1,0:T(8,128)S(1)}, u32[]{:S(2)}, u32[]{:S(2)}) collective-permute-start(f32[16,8,512]{2,1,0:T(8,128)S(1)} %fusion.76), channel_id=1, source_target_pairs={{0,16},{16,32},{32,48},{48,64},{64,80},{80,96},{96,112},{112,128},... | collective-permute-start | bytes 786440 | tf_op jit(solution)/shard_map/while/body/eval_jaxpr/ppermute | solution.py:33
  225.3 6.8 %collective-permute-start = (f32[16,1,512]{2,1,0:T(1,128)S(1)}, f32[16,1,512]{2,1,0:T(1,128)S(1)}, u32[]{:S(2)}, u32[]{:S(2)}) collective-permute-start(f32[16,1,512]{2,1,0:T(1,128)S(1)} %get-tuple-element.211), channel_id=1, source_target_pairs={{1,0},{2,1},{3,2},{4,3},{5,4},{6,5},{7,6},{8,7},{9,8},{10,9},{11,1... | collective-permute-start | bytes 98312 | tf_op jit(solution)/shard_map/while/body/eval_jaxpr/ppermute | solution.py:23
  228.2 4.9 %collective-permute-start.1 = (f32[16,1,512]{2,1,0:T(1,128)S(1)}, f32[16,1,512]{2,1,0:T(1,128)S(1)}, u32[]{:S(2)}, u32[]{:S(2)}) collective-permute-start(f32[16,1,512]{2,1,0:T(1,128)S(1)} %get-tuple-element.212), channel_id=1, source_target_pairs={{0,1},{1,2},{2,3},{3,4},{4,5},{5,6},{6,7},{7,8},{8,9},{9,10},{10,1... | collective-permute-start | bytes 98312 | tf_op jit(solution)/shard_map/while/body/eval_jaxpr/ppermute | solution.py:21
  233.9 11.6 %collective-permute-start.2 = (f32[16,8,512]{2,1,0:T(8,128)S(1)}, f32[16,8,512]{2,1,0:T(8,128)S(1)}, u32[]{:S(2)}, u32[]{:S(2)}) collective-permute-start(f32[16,8,512]{2,1,0:T(8,128)S(1)} %fusion.76), channel_id=1, source_target_pairs={{0,16},{16,32},{32,48},{48,64},{64,80},{80,96},{96,112},{112,128},... | collective-permute-start | bytes 786440 | tf_op jit(solution)/shard_map/while/body/eval_jaxpr/ppermute | solution.py:33
  245.6 6.8 %collective-permute-start = (f32[16,1,512]{2,1,0:T(1,128)S(1)}, f32[16,1,512]{2,1,0:T(1,128)S(1)}, u32[]{:S(2)}, u32[]{:S(2)}) collective-permute-start(f32[16,1,512]{2,1,0:T(1,128)S(1)} %get-tuple-element.211), channel_id=1, source_target_pairs={{1,0},{2,1},{3,2},{4,3},{5,4},{6,5},{7,6},{8,7},{9,8},{10,9},{11,1... | collective-permute-start | bytes 98312 | tf_op jit(solution)/shard_map/while/body/eval_jaxpr/ppermute | solution.py:23
  248.7 4.7 %collective-permute-start.1 = (f32[16,1,512]{2,1,0:T(1,128)S(1)}, f32[16,1,512]{2,1,0:T(1,128)S(1)}, u32[]{:S(2)}, u32[]{:S(2)}) collective-permute-start(f32[16,1,512]{2,1,0:T(1,128)S(1)} %get-tuple-element.212), channel_id=1, source_target_pairs={{0,1},{1,2},{2,3},{3,4},{4,5},{5,6},{6,7},{7,8},{8,9},{9,10},{10,1... | collective-permute-start | bytes 98312 | tf_op jit(solution)/shard_map/while/body/eval_jaxpr/ppermute | solution.py:21
  254.2 11.3 %collective-permute-start.2 = (f32[16,8,512]{2,1,0:T(8,128)S(1)}, f32[16,8,512]{2,1,0:T(8,128)S(1)}, u32[]{:S(2)}, u32[]{:S(2)}) collective-permute-start(f32[16,8,512]{2,1,0:T(8,128)S(1)} %fusion.76), channel_id=1, source_target_pairs={{0,16},{16,32},{32,48},{48,64},{64,80},{80,96},{96,112},{112,128},... | collective-permute-start | bytes 786440 | tf_op jit(solution)/shard_map/while/body/eval_jaxpr/ppermute | solution.py:33
  265.7 6.8 %collective-permute-start = (f32[16,1,512]{2,1,0:T(1,128)S(1)}, f32[16,1,512]{2,1,0:T(1,128)S(1)}, u32[]{:S(2)}, u32[]{:S(2)}) collective-permute-start(f32[16,1,512]{2,1,0:T(1,128)S(1)} %get-tuple-element.211), channel_id=1, source_target_pairs={{1,0},{2,1},{3,2},{4,3},{5,4},{6,5},{7,6},{8,7},{9,8},{10,9},{11,1... | collective-permute-start | bytes 98312 | tf_op jit(solution)/shard_map/while/body/eval_jaxpr/ppermute | solution.py:23
  269.0 4.5 %collective-permute-start.1 = (f32[16,1,512]{2,1,0:T(1,128)S(1)}, f32[16,1,512]{2,1,0:T(1,128)S(1)}, u32[]{:S(2)}, u32[]{:S(2)}) collective-permute-start(f32[16,1,512]{2,1,0:T(1,128)S(1)} %get-tuple-element.212), channel_id=1, source_target_pairs={{0,1},{1,2},{2,3},{3,4},{4,5},{5,6},{6,7},{7,8},{8,9},{9,10},{10,1... | collective-permute-start | bytes 98312 | tf_op jit(solution)/shard_map/while/body/eval_jaxpr/ppermute | solution.py:21
  274.3 11.1 %collective-permute-start.2 = (f32[16,8,512]{2,1,0:T(8,128)S(1)}, f32[16,8,512]{2,1,0:T(8,128)S(1)}, u32[]{:S(2)}, u32[]{:S(2)}) collective-permute-start(f32[16,8,512]{2,1,0:T(8,128)S(1)} %fusion.76), channel_id=1, source_target_pairs={{0,16},{16,32},{32,48},{48,64},{64,80},{80,96},{96,112},{112,128},... | collective-permute-start | bytes 786440 | tf_op jit(solution)/shard_map/while/body/eval_jaxpr/ppermute | solution.py:33
  285.5 6.8 %collective-permute-start = (f32[16,1,512]{2,1,0:T(1,128)S(1)}, f32[16,1,512]{2,1,0:T(1,128)S(1)}, u32[]{:S(2)}, u32[]{:S(2)}) collective-permute-start(f32[16,1,512]{2,1,0:T(1,128)S(1)} %get-tuple-element.211), channel_id=1, source_target_pairs={{1,0},{2,1},{3,2},{4,3},{5,4},{6,5},{7,6},{8,7},{9,8},{10,9},{11,1... | collective-permute-start | bytes 98312 | tf_op jit(solution)/shard_map/while/body/eval_jaxpr/ppermute | solution.py:23
  294.1 10.8 %collective-permute-start.2 = (f32[16,8,512]{2,1,0:T(8,128)S(1)}, f32[16,8,512]{2,1,0:T(8,128)S(1)}, u32[]{:S(2)}, u32[]{:S(2)}) collective-permute-start(f32[16,8,512]{2,1,0:T(8,128)S(1)} %fusion.76), channel_id=1, source_target_pairs={{0,16},{16,32},{32,48},{48,64},{64,80},{80,96},{96,112},{112,128},... | collective-permute-start | bytes 786440 | tf_op jit(solution)/shard_map/while/body/eval_jaxpr/ppermute | solution.py:33
  305.0 7.0 %collective-permute-start = (f32[16,1,512]{2,1,0:T(1,128)S(1)}, f32[16,1,512]{2,1,0:T(1,128)S(1)}, u32[]{:S(2)}, u32[]{:S(2)}) collective-permute-start(f32[16,1,512]{2,1,0:T(1,128)S(1)} %get-tuple-element.211), channel_id=1, source_target_pairs={{1,0},{2,1},{3,2},{4,3},{5,4},{6,5},{7,6},{8,7},{9,8},{10,9},{11,1... | collective-permute-start | bytes 98312 | tf_op jit(solution)/shard_map/while/body/eval_jaxpr/ppermute | solution.py:23
  313.8 10.7 %collective-permute-start.2 = (f32[16,8,512]{2,1,0:T(8,128)S(1)}, f32[16,8,512]{2,1,0:T(8,128)S(1)}, u32[]{:S(2)}, u32[]{:S(2)}) collective-permute-start(f32[16,8,512]{2,1,0:T(8,128)S(1)} %fusion.76), channel_id=1, source_target_pairs={{0,16},{16,32},{32,48},{48,64},{64,80},{80,96},{96,112},{112,128},... | collective-permute-start | bytes 786440 | tf_op jit(solution)/shard_map/while/body/eval_jaxpr/ppermute | solution.py:33
  324.6 7.1 %collective-permute-start = (f32[16,1,512]{2,1,0:T(1,128)S(1)}, f32[16,1,512]{2,1,0:T(1,128)S(1)}, u32[]{:S(2)}, u32[]{:S(2)}) collective-permute-start(f32[16,1,512]{2,1,0:T(1,128)S(1)} %get-tuple-element.211), channel_id=1, source_target_pairs={{1,0},{2,1},{3,2},{4,3},{5,4},{6,5},{7,6},{8,7},{9,8},{10,9},{11,1... | collective-permute-start | bytes 98312 | tf_op jit(solution)/shard_map/while/body/eval_jaxpr/ppermute | solution.py:23
  333.5 10.7 %collective-permute-start.2 = (f32[16,8,512]{2,1,0:T(8,128)S(1)}, f32[16,8,512]{2,1,0:T(8,128)S(1)}, u32[]{:S(2)}, u32[]{:S(2)}) collective-permute-start(f32[16,8,512]{2,1,0:T(8,128)S(1)} %fusion.76), channel_id=1, source_target_pairs={{0,16},{16,32},{32,48},{48,64},{64,80},{80,96},{96,112},{112,128},... | collective-permute-start | bytes 786440 | tf_op jit(solution)/shard_map/while/body/eval_jaxpr/ppermute | solution.py:33
  344.3 7.1 %collective-permute-start = (f32[16,1,512]{2,1,0:T(1,128)S(1)}, f32[16,1,512]{2,1,0:T(1,128)S(1)}, u32[]{:S(2)}, u32[]{:S(2)}) collective-permute-start(f32[16,1,512]{2,1,0:T(1,128)S(1)} %get-tuple-element.211), channel_id=1, source_target_pairs={{1,0},{2,1},{3,2},{4,3},{5,4},{6,5},{7,6},{8,7},{9,8},{10,9},{11,1... | collective-permute-start | bytes 98312 | tf_op jit(solution)/shard_map/while/body/eval_jaxpr/ppermute | solution.py:23
  353.2 10.7 %collective-permute-start.2 = (f32[16,8,512]{2,1,0:T(8,128)S(1)}, f32[16,8,512]{2,1,0:T(8,128)S(1)}, u32[]{:S(2)}, u32[]{:S(2)}) collective-permute-start(f32[16,8,512]{2,1,0:T(8,128)S(1)} %fusion.76), channel_id=1, source_target_pairs={{0,16},{16,32},{32,48},{48,64},{64,80},{80,96},{96,112},{112,128},... | collective-permute-start | bytes 786440 | tf_op jit(solution)/shard_map/while/body/eval_jaxpr/ppermute | solution.py:33
  364.0 7.1 %collective-permute-start = (f32[16,1,512]{2,1,0:T(1,128)S(1)}, f32[16,1,512]{2,1,0:T(1,128)S(1)}, u32[]{:S(2)}, u32[]{:S(2)}) collective-permute-start(f32[16,1,512]{2,1,0:T(1,128)S(1)} %get-tuple-element.211), channel_id=1, source_target_pairs={{1,0},{2,1},{3,2},{4,3},{5,4},{6,5},{7,6},{8,7},{9,8},{10,9},{11,1... | collective-permute-start | bytes 98312 | tf_op jit(solution)/shard_map/while/body/eval_jaxpr/ppermute | solution.py:23
  372.9 10.7 %collective-permute-start.2 = (f32[16,8,512]{2,1,0:T(8,128)S(1)}, f32[16,8,512]{2,1,0:T(8,128)S(1)}, u32[]{:S(2)}, u32[]{:S(2)}) collective-permute-start(f32[16,8,512]{2,1,0:T(8,128)S(1)} %fusion.76), channel_id=1, source_target_pairs={{0,16},{16,32},{32,48},{48,64},{64,80},{80,96},{96,112},{112,128},... | collective-permute-start | bytes 786440 | tf_op jit(solution)/shard_map/while/body/eval_jaxpr/ppermute | solution.py:33
  383.8 7.1 %collective-permute-start.10 = (f32[16,1,512]{2,0,1:T(8,128)S(1)}, f32[16,1,512]{2,0,1:T(8,128)S(1)}, u32[]{:S(2)}, u32[]{:S(2)}) collective-permute-start(f32[16,1,512]{2,0,1:T(8,128)S(1)} %get-tuple-element.173), channel_id=1, source_target_pairs={{0,1},{1,2},{2,3},{3,4},{4,5},{5,6},{6,7},{7,8},{8,9},{9,10},{10,1... | collective-permute-start | bytes 98312 | tf_op jit(solution)/shard_map/ppermute | solution.py:21
  389.0 6.4 %collective-permute-start.9 = (f32[16,1,512]{2,0,1:T(8,128)S(1)}, f32[16,1,512]{2,0,1:T(8,128)S(1)}, u32[]{:S(2)}, u32[]{:S(2)}) collective-permute-start(f32[16,1,512]{2,0,1:T(8,128)S(1)} %get-tuple-element.174), channel_id=1, source_target_pairs={{1,0},{2,1},{3,2},{4,3},{5,4},{6,5},{7,6},{8,7},{9,8},{10,9},{11,1... | collective-permute-start | bytes 98312 | tf_op jit(solution)/shard_map/ppermute | solution.py:23
  (11 other events, 65.6 us)
where the time goes:
time: 415 us; the launch traced here: 413 us
  starting transfers between devices  159 us (38%)
  waiting for transfers between devices  157 us (38%)
  other arithmetic  54.6 us (13%)
  local copies, waits for them, and re-layouts  39.8 us (10%)
    ppermute x15, waiting for transfers between devices, from_behind(): return lax.ppermute(block, axis, route)  137 us
    ppermute x19, starting transfers between devices, extended(): lax.ppermute(tail, axis, [(i, (i + 1) % count) for i in range(ends)])  76.9 us
    ppermute x19, starting transfers between devices, extended(): lax.ppermute(head, axis, [((i + 1) % count, i) for i in range(ends)])  52.2 us
    reduce_sum x3, other arithmetic, restrict(): return 0.25 * jnp.sum(blocks, axis=(2, 4))  31 us
    ppermute x15, starting transfers between devices, from_behind(): return lax.ppermute(block, axis, route)  30 us
    ppermute x19, waiting for transfers between devices, extended(): lax.ppermute(tail, axis, [(i, (i + 1) % count) for i in range(ends)])  14.9 us
    unnamed x14, local copies, waits for them, and re-layouts  10.6 us
    concatenate x20, other arithmetic, extended(): jnp.concatenate([lax.ppermute(tail, axis, [(i, (i + 1) % count) for i in...  9.37 us
  transfers between devices with their start and end apart: 53, of which 31 were waited for; matrix products, arithmetic and copies ran while one was open for 10% of the time, Pallas kernels for 0%

commit v1 on v0

v1 whole, which is shorter than its diff:
```python
import jax
import jax.numpy as jnp
from jax import lax
from jax.experimental import pallas as pl
from jax.experimental.pallas import tpu as pltpu
from jax.sharding import PartitionSpec as P

Z = 16
X = 16
Y = 1024
T = 16
S = 16
CX = X // 2
CY = Y // 2
ROWS = Z * X
CROWS = Z * CX
OWN = CY // T
MARGIN = 16
HALF = Z // 2
FIRST = 7
SPAN = 3 * CX

DIFFUSE = 0.15
REACTION = 0.1
VMEM_LIMIT = 48 * 1024 * 1024
PACK_VMEM = 54272 * 1024


MOBILITY = T
EARLY = (
    ((0, 7), (6, 1)),
    ((1, 6), (5, 2)),
    ((2, 5), (4, 3)),
    ((3, 4), (MOBILITY, 4)),
)
LATE = (
    ((8, 7), (14, 1)),
    ((9, 6), (13, 2)),
    ((10, 5), (12, 3)),
)
LAST = 11
EARLY_TILES = len(EARLY) * HALF + 2
LATE_TILES = (len(LATE) + 1) * HALF


def call(body, outs, scratch=(), flops=0):
    return pl.pallas_call(
        body,
        out_shape=[jax.ShapeDtypeStruct(shape, jnp.float32) for shape in outs],
        scratch_shapes=[pltpu.VMEM(shape, jnp.float32) for shape in scratch],
        compiler_params=pltpu.CompilerParams(vmem_limit_bytes=VMEM_LIMIT),
        cost_estimate=pl.CostEstimate(flops=flops, bytes_accessed=4_000_000, transcendentals=0),
    )


def iota(shape, axis):
    return lax.broadcasted_iota(jnp.int32, shape, axis)


def split(value):
    high = value.astype(jnp.bfloat16)
    low = (value - high.astype(jnp.float32)).astype(jnp.bfloat16)
    return high, low


def restrict(value, parts):
    high, low = split(value)
    pick = (iota((256, 128), 0) // 2 == iota((256, 128), 1)).astype(jnp.bfloat16)
    for k in range(Y // 256):
        chunk = slice(256 * k, 256 * (k + 1))
        parts[k] = jnp.dot(high[:, chunk], pick, preferred_element_type=jnp.float32) + jnp.dot(
            low[:, chunk], pick, preferred_element_type=jnp.float32
        )
    pieces = [
        parts[k, pl.ds(0, CROWS, stride=2), :] + parts[k, pl.ds(1, CROWS, stride=2), :]
        for k in range(Y // 256)
    ]
    return 0.25 * jnp.concatenate(pieces, axis=1)


def halve_lanes(value):
    high, low = split(value)
    pick = (iota((256, 128), 0) // 2 == iota((256, 128), 1)).astype(jnp.bfloat16)
    pieces = []
    for k in range(Y // 256):
        chunk = slice(256 * k, 256 * (k + 1))
        pieces.append(
            jnp.dot(high[:, chunk], pick, preferred_element_type=jnp.float32)
            + jnp.dot(low[:, chunk], pick, preferred_element_type=jnp.float32)
        )
    return jnp.concatenate(pieces, axis=1)


def beside_lanes(value):
    count = value.shape[-1]
    axis = value.ndim - 1
    before = pltpu.roll(value, 1, axis)
    after = pltpu.roll(value, count - 1, axis)
    lane = iota(value.shape[:-1] + (128,), axis)
    before = jnp.concatenate(
        [jnp.where(lane == 0, 0.0, before[..., :128]), before[..., 128:]], axis=axis
    )
    after = jnp.concatenate(
        [after[..., :-128], jnp.where(lane == 127, 0.0, after[..., -128:])], axis=axis
    )
    return before + after


def fine_rule(center, around, mobility):
    return DIFFUSE * around + REACTION * (center * (1.0 + mobility * (1.0 - center * center)))


def fine_tile(ref, mob_ref, z, tile, low_row, high_row):
    base = z * X + tile * 8
    center = ref[pl.ds(base, 8), :]
    row = iota((8, Y), 0)
    below = ref[pl.ds(base - 1, 1), :] if tile else low_row
    above = high_row if tile else ref[pl.ds(base + 8, 1), :]
    around = jnp.where(row == 0, below, pltpu.roll(center, 1, 0))
    around += jnp.where(row == 7, above, pltpu.roll(center, 7, 0))
    around += beside_lanes(center)
    if z > 0:
        around += ref[pl.ds(base - X, 8), :]
    if z < Z - 1:
        around += ref[pl.ds(base + X, 8), :]
    return fine_rule(center, around, mob_ref[pl.ds(base, 8), :])


def pack_fine_body(iterate, mobility, odd, even, done):
    space = lax.axis_index("space")

    def put(low, high):
        moves = []
        for out, near, far in ((low, 0, 1), (high, X - 1, X - 2)):
            for k, (source, inner) in enumerate(((iterate, near), (iterate, far), (mobility, near))):
                moves.append(
                    pltpu.make_async_copy(source.at[:, inner, :], out.at[k], done.at[len(moves)])
                )
        for move in moves:
            move.start()
        for move in moves:
            move.wait()

    pl.when(space % 2 == 0)(lambda: put(odd, even))
    pl.when(space % 2 == 1)(lambda: put(even, odd))


def windows(value):
    count = CY // 128
    blank = jnp.zeros((HALF, CX, 128), jnp.float32)
    lane = iota((HALF, CX, 128), 2)
    moved = {}

    def piece(half, index, amount):
        if not 0 <= index < count:
            return blank
        if (half, index, amount) not in moved:
            planes = value[HALF * half : HALF * (half + 1)]
            moved[half, index, amount] = pltpu.roll(
                planes[:, :, 128 * index : 128 * (index + 1)], amount, 2
            )
        return moved[half, index, amount]

    tiles = []
    for tile in range(T):
        start = tile * OWN - MARGIN
        first = start // 128
        offset = start - first * 128
        parts = []
        for half in range(2):
            amount = (64 * half - offset) % 128
            part = piece(half, first, amount)
            if offset + 64 > 128:
                after = piece(half, first + 1, amount)
                part = jnp.where(lane < 64 * half + 128 - offset, part, after)
            parts.append(part)
        tiles.append(jnp.where(lane < 64, parts[0], parts[1]))
    return tiles


def turned(value, tile):
    start = tile * OWN - MARGIN
    wide = jnp.concatenate([value, jnp.zeros((Z, CX, 128), jnp.float32)], axis=2)
    count = CY + 128
    first = pltpu.roll(wide[:HALF], (count - start) % count, 2)[:, :, :128]
    second = pltpu.roll(wide[HALF:], (count - start + 64) % count, 2)[:, :, :128]
    return jnp.where(iota((HALF, CX, 128), 2) < 64, first, second)


def partial_step(source, mobility, target):
    none = jnp.zeros((1, Y), jnp.float32)
    for z in range(Z):
        for tile in range(X // 8):
            target[pl.ds(z * X + tile * 8, 8), :] = fine_tile(
                source, mobility, z, tile, none, none
            )


def before_body(pending, iterate, mobility, stepped, coarse_old, mob_tile, outer, flag, parts):
    turn = lax.axis_index("tm")
    mine = jnp.where(iota((1, T), 1) == turn, pending[...], 0)
    chosen = jnp.sum(mine, axis=1, keepdims=True)
    flag[...] = jnp.broadcast_to(jnp.where(chosen > 0, 1.0, 0.0), (8, 128))
    partial_step(iterate, mobility, stepped)
    for side, inner in ((0, 0), (1, X - 1)):
        for z in range(Z):
            outer[side, pl.ds(z, 1), :] = stepped[pl.ds(z * X + inner, 1), :]
    coarse_mobility = restrict(mobility[...], parts).reshape(Z, CX, CY)
    start = restrict(iterate[...], parts).reshape(Z, CX, CY)
    row = iota((Z, CX, CY), 1)
    around = jnp.where(row == 0, 0.0, pltpu.roll(start, 1, 1))
    around += jnp.where(row == CX - 1, 0.0, pltpu.roll(start, CX - 1, 1))
    around += beside_lanes(start)
    flat = jnp.zeros((1, CX, CY), jnp.float32)
    stacked = jnp.concatenate([start[1:], flat], axis=0)
    stacked += jnp.concatenate([flat, start[:-1]], axis=0)
    rate = 2.0 * REACTION * coarse_mobility
    kept, given = coarse_rule(start, 0.5 * DIFFUSE * around, stacked, rate)
    coarse_old[...] = (kept + given).reshape(CROWS, CY)
    mob_tile[...] = turned(coarse_mobility, turn)


def second_body(flag, stepped, mobility, coarse_old, previous, fine, sent, parts):
    turn = lax.axis_index("tm")
    flagged = jnp.max(flag[...]) > 0.5
    pl.when(flagged)(lambda: partial_step(stepped, mobility, fine))

    @pl.when(jnp.logical_not(flagged))
    def _():
        fine[...] = previous[...]

    weight = jnp.where(turn > 0, 1.0, 0.0)
    term = restrict(fine[...], parts) - weight * coarse_old[...]
    for tile, value in enumerate(windows(term.reshape(Z, CX, CY))):
        sent[tile] = value


def coarse_rule(center, beside, stacked, rate):
    bottom = 1.0 + rate * (center * center)
    inverse = pltpu.reciprocal(bottom, approx=True)
    inverse = inverse * (2.0 - bottom * inverse)
    kept = center * ((1.0 + rate) * inverse - 6.0 * DIFFUSE)
    return kept, beside + 2.0 * DIFFUSE * stacked


def edge_windows(value):
    count = CY // 128
    lane = iota((HALF, 128), 1)
    moved = {}

    def piece(half, index, amount):
        if not 0 <= index < count:
            return jnp.zeros((HALF, 128), jnp.float32)
        if (half, index, amount) not in moved:
            part = value[HALF * half : HALF * (half + 1), 128 * index : 128 * (index + 1)]
            moved[half, index, amount] = pltpu.roll(part, amount, 1)
        return moved[half, index, amount]

    tiles = []
    for tile in range(T):
        start = tile * OWN - MARGIN
        first = start // 128
        offset = start - first * 128
        parts = []
        for half in range(2):
            amount = (64 * half - offset) % 128
            part = piece(half, first, amount)
            if offset + 64 > 128:
                after = piece(half, first + 1, amount)
                part = jnp.where(lane < 64 * half + 128 - offset, part, after)
            parts.append(part)
        tiles.append(jnp.where(lane < 64, parts[0], parts[1]))
    return tiles


def edge_body(
    flag, own_odd, own_even, odd, even, outer, sent_in, sent, change, old_change, halo, added_rows
):
    space = lax.axis_index("space")
    turn = lax.axis_index("tm")

    def take(low, high, own_low, own_high):
        for side, (got, own) in enumerate(((low, own_low), (high, own_high))):
            for k in range(3):
                halo[side, k] = got[k]
            halo[side, 3] = own[0]
            halo[side, 4] = own[2]

    pl.when(space % 2 == 0)(lambda: take(odd, even, own_odd, own_even))
    pl.when(space % 2 == 1)(lambda: take(even, odd, own_even, own_odd))

    flagged = flag[pl.ds(0, 1), pl.ds(0, 1)]
    weight = jnp.where(turn > 0, 1.0, 0.0)
    plane = iota((Z, Y), 0)

    def beside(value):
        total = jnp.where(plane == 0, 0.0, pltpu.roll(value, 1, 0))
        total += jnp.where(plane == Z - 1, 0.0, pltpu.roll(value, Z - 1, 0))
        return total + beside_lanes(value)

    sums = [None] * 4
    for side, inside in ((0, space > 0), (1, space < S - 1)):
        keep = jnp.where(inside, 1.0, 0.0)
        near, far, mob = keep * halo[side, 0], keep * halo[side, 1], halo[side, 2]
        own, own_mob = halo[side, 3], halo[side, 4]
        beyond = keep * fine_rule(near, far + own + beside(near), mob)
        added = DIFFUSE * near
        before = outer[side]
        after = before + added
        grown = after * (1.0 - after * after) - before * (1.0 - before * before)
        first = added + DIFFUSE * (beyond + beside(added) - 6.0 * added)
        first = flagged * (first + REACTION * own_mob * grown)
        second = flagged * DIFFUSE * added
        change[side, 0] = first
        change[side, 1] = second
        sums[side] = near + far
        sums[2 + side] = first + second
    halved = halve_lanes(jnp.concatenate(sums, axis=0))
    for side in range(2):
        coarse_side = (0.5 * DIFFUSE * 0.25) * halved[side * Z : (side + 1) * Z]
        fine_side = 0.25 * halved[(2 + side) * Z : (3 + side) * Z]
        old_change[side] = coarse_side
        for tile, value in enumerate(edge_windows(fine_side - weight * coarse_side)):
            added_rows[side, tile] = value
    row = iota((CX, 128), 0)
    for tile in range(T):
        for z in range(HALF):
            low = added_rows[0, tile, pl.ds(z, 1), :]
            high = added_rows[1, tile, pl.ds(z, 1), :]
            change_here = jnp.where(row == 0, low, jnp.where(row == CX - 1, high, 0.0))
            sent[tile, z] = sent_in[tile, z] + change_here


def repair_body(fine_in, change, old_in, old_change, fine, coarse_old):
    row = iota((8, Y), 0)
    coarse_row = iota((CX, CY), 0)
    for z in range(Z):
        for side in range(2):
            here = pl.ds(z * X + side * 8, 8)
            first = change[side, 0, pl.ds(z, 1), :]
            second = change[side, 1, pl.ds(z, 1), :]
            last = 7 * side
            added = jnp.where(row == last, first, jnp.where(row == abs(last - 1), second, 0.0))
            fine[here, :] = fine_in[here, :] + added
        here = pl.ds(z * CX, CX)
        low, high = old_change[0, pl.ds(z, 1), :], old_change[1, pl.ds(z, 1), :]
        added = jnp.where(coarse_row == 0, low, jnp.where(coarse_row == CX - 1, high, 0.0))
        coarse_old[here, :] = old_in[here, :] + added


def pack_chain_body(terms, mob_tile, odd, even, late_odd, late_even):
    space = lax.axis_index("space")
    row = iota((HALF, CX, 128), 1)

    def of(number):
        return mob_tile[...] if number == MOBILITY else terms[number]

    def put(low, high, late_low, late_high):
        for pairs, first, last in ((EARLY, low, high), (LATE, late_low, late_high)):
            for k, ((one, rows), (other, rest)) in enumerate(pairs):
                here, there = of(one), of(other)
                place = pl.ds(k * HALF, HALF)
                first[place] = jnp.where(row < rows, here, pltpu.roll(there, rows, 1))
                last[place] = jnp.where(row >= rest, here, pltpu.roll(there, rest, 1))
        for k in range(2):
            for z in range(HALF):
                low[EARLY_TILES - 2 + k, pl.ds(z, 1), :] = mob_tile[z, pl.ds(4 + k, 1), :]
                high[EARLY_TILES - 2 + k, pl.ds(z, 1), :] = mob_tile[z, pl.ds(2 + k, 1), :]
        place = pl.ds(len(LATE) * HALF, HALF)
        late_low[place] = jnp.where(row < 4, terms[LAST], mob_tile[...])
        late_high[place] = jnp.where(row >= 4, terms[LAST], mob_tile[...])

    pl.when(space % 2 == 0)(lambda: put(odd, even, late_odd, late_even))
    pl.when(space % 2 == 1)(lambda: put(even, odd, late_even, late_odd))


def chain_parts(terms, shipments):
    place = {}
    for pairs, low, high in shipments:
        for k, ((one, rows), (other, rest)) in enumerate(pairs):
            place[one] = (low, high, k, 0, 0)
            place[other] = (low, high, k, CX - rest, CX - rows)

    def extended(number):
        own = terms[number]
        if number not in place:
            return jnp.concatenate([jnp.zeros_like(own), own, jnp.zeros_like(own)], axis=1)
        low, high, k, up, down = place[number]
        below, above = low[pl.ds(k * HALF, HALF)], high[pl.ds(k * HALF, HALF)]
        if up:
            below = pltpu.roll(below, up, 1)
            above = pltpu.roll(above, down, 1)
        return jnp.concatenate([below, own, above], axis=1)

    return extended


def inner_mobility(low, high):
    place = pl.ds((len(EARLY) - 1) * HALF, HALF)
    return pltpu.roll(low[place], 4, 1), pltpu.roll(high[place], 4, 1)


def early_mobility(low, high):
    below, above = inner_mobility(low, high)
    row = iota((CX, 128), 0)
    lows, highs = [], []
    for z in range(HALF):
        low_rows = [low[EARLY_TILES - 2 + k, pl.ds(z, 1), :] for k in range(2)]
        high_rows = [high[EARLY_TILES - 2 + k, pl.ds(z, 1), :] for k in range(2)]
        outer = jnp.where(row == 2, low_rows[0], jnp.where(row == 3, low_rows[1], 0.0))
        lows.append(jnp.where(row >= 4, below[z], outer)[None])
        outer = jnp.where(row == 4, high_rows[0], jnp.where(row == 5, high_rows[1], 0.0))
        highs.append(jnp.where(row < 4, above[z], outer)[None])
    return jnp.concatenate(lows, axis=0), jnp.concatenate(highs, axis=0)


def late_mobility(low, high, late_low, late_high):
    below, above = inner_mobility(low, high)
    place = pl.ds(len(LATE) * HALF, HALF)
    row = iota((HALF, CX, 128), 1)
    return (
        jnp.where(row >= 4, below, late_low[place]),
        jnp.where(row < 4, above, late_high[place]),
    )


def around_chain(space, turn):
    row = iota((1, SPAN, 128), 1) - CX + space * CX
    column = iota((1, SPAN, 128), 2) % 64 - MARGIN + turn * OWN
    inside = (row >= 0) & (row < S * CX) & (column >= 0) & (column < CY)
    return jnp.where(inside, 0.5 * DIFFUSE, 0.0)


def chain_step(state, rate, weight):
    lane = iota((1, SPAN, 128), 2)
    crossed_up = jnp.where(lane < 64, pltpu.roll(state[:1], 64, 2), 0.0)
    crossed_down = jnp.where(lane >= 64, pltpu.roll(state[HALF - 1 :], 64, 2), 0.0)
    stacked = jnp.concatenate([state[1:], crossed_up], axis=0)
    stacked += jnp.concatenate([crossed_down, state[:-1]], axis=0)
    beside = pltpu.roll(state, 1, 1) + pltpu.roll(state, SPAN - 1, 1)
    beside += pltpu.roll(state, 1, 2) + pltpu.roll(state, 127, 2)
    return coarse_rule(state, weight * beside, stacked, rate)


def returned(advanced):
    own = advanced[:, CX : 2 * CX, :]
    lane = iota((4, CX, 128), 2)
    return jnp.where(
        lane % 64 < OWN,
        pltpu.roll(own[:4], 128 - MARGIN, 2),
        pltpu.roll(own[4:], OWN - MARGIN, 2),
    )


def run_chain(state, extended, rate, weight, numbers, back):
    for number in numbers:
        kept, given = chain_step(state, rate, weight)
        back[number] = returned(kept + given)
        if number < T - 1:
            state = kept + (given + extended(number))
    return state


def receive(odd, even, low, high):
    space = lax.axis_index("space")

    def take(one, other):
        low[...] = jnp.where(space > 0, one[...], 0.0)
        high[...] = jnp.where(space < S - 1, other[...], 0.0)

    pl.when(space % 2 == 0)(lambda: take(odd, even))
    pl.when(space % 2 == 1)(lambda: take(even, odd))


def chain_rate(below, mob_tile, above):
    return (2.0 * REACTION) * jnp.concatenate([below, mob_tile[...], above], axis=1)


def chain_one_body(terms, mob_tile, odd, even, back, middle, low, high):
    receive(odd, even, low, high)
    extended = chain_parts(terms, [(EARLY, low, high)])
    below, above = early_mobility(low, high)
    rate = chain_rate(below, mob_tile, above)
    weight = around_chain(lax.axis_index("space"), lax.axis_index("tm"))
    back[0] = jnp.zeros((4, CX, 128), jnp.float32)
    state = run_chain(extended(0), extended, rate, weight, range(1, FIRST + 1), back)
    middle[...] = state[:, CX : 2 * CX, :]


def chain_two_body(
    terms, mob_tile, odd, even, late_odd, late_even, first, middle, mid_odd, mid_even,
    back, low, high, late_low, late_high, below, above,
):
    receive(odd, even, low, high)
    receive(late_odd, late_even, late_low, late_high)
    receive(mid_odd, mid_even, below, above)
    late = LATE + (((LAST, 4), (MOBILITY, 4)),)
    extended = chain_parts(terms, [(EARLY, low, high), (late, late_low, late_high)])
    mob_below, mob_above = late_mobility(low, high, late_low, late_high)
    rate = chain_rate(mob_below, mob_tile, mob_above)
    weight = around_chain(lax.axis_index("space"), lax.axis_index("tm"))
    back[pl.ds(0, FIRST + 1)] = first[...]
    state = jnp.concatenate([below[...], middle[...], above[...]], axis=1)
    run_chain(state, extended, rate, weight, range(FIRST + 1, T), back)


def finish_body(fine, coarse_old, arrived, out_far, parts, out, done):
    turn = lax.axis_index("tm")
    lane = iota((CX, 128), 1)
    weight = jnp.where(turn > 0, 1.0, 0.0)
    pick = (iota((256, 256), 0) % 128 == iota((256, 256), 1) // 2).astype(jnp.bfloat16)
    stores = []
    deep = Z // 4
    few, many = deep * CX, deep * X
    chunks = CY // 128
    for group in range(4):
        for part in range(chunks):
            planes = []
            for quarter in range(4):
                total = None
                for k in range(4):
                    block = arrived[4 * part + k, quarter]
                    shift = (OWN * (k - group)) % 128
                    block = pltpu.roll(block, shift, 1) if shift else block
                    total = block if total is None else jnp.where(lane >= OWN * k, block, total)
                planes.append(total)
            advanced = jnp.concatenate(planes, axis=0)
            old = coarse_old[pl.ds(group * few, few), pl.ds(128 * part, 128)]
            both = jnp.concatenate(split(weight * (advanced - old)), axis=1)
            wide = jnp.dot(both, pick, preferred_element_type=jnp.float32)
            for half in range(2):
                block = wide[:, 128 * half : 128 * (half + 1)]
                start = (2 * part + half) * many
                parts[group, pl.ds(start, few, stride=2), :] = block
                parts[group, pl.ds(start + 1, few, stride=2), :] = block
        rows = pl.ds(group * many, many)
        for part in range(2 * chunks):
            columns = pl.ds(128 * part, 128)
            out[rows, columns] = fine[rows, columns] + parts[group, pl.ds(part * many, many), :]
        stores.append(
            pltpu.make_async_copy(out.at[rows, :], out_far.at[rows, :], done.at[group])
        )
        stores[-1].start()
    for store in stores:
        store.wait()


def pack_fine(iterate, mobility):
    rows = jax.ShapeDtypeStruct((3, Z, Y), jnp.float32)
    return pl.pallas_call(
        pack_fine_body,
        out_shape=[rows, rows],
        in_specs=[pl.BlockSpec(memory_space=pltpu.HBM)] * 2,
        out_specs=[pl.BlockSpec(memory_space=pltpu.VMEM)] * 2,
        scratch_shapes=[pltpu.SemaphoreType.DMA((6,))],
        compiler_params=pltpu.CompilerParams(vmem_limit_bytes=PACK_VMEM),
        cost_estimate=pl.CostEstimate(flops=0, bytes_accessed=400_000, transcendentals=0),
    )(iterate, mobility)


def finish(fine, coarse_old, arrived):
    return pl.pallas_call(
        finish_body,
        out_shape=jax.ShapeDtypeStruct((ROWS, Y), jnp.float32),
        in_specs=[pl.BlockSpec(memory_space=pltpu.VMEM)] * 3,
        out_specs=pl.BlockSpec(memory_space=pltpu.HBM),
        scratch_shapes=[
            pltpu.VMEM((4, Y // 128 * X * Z // 4, 128), jnp.float32),
            pltpu.VMEM((ROWS, Y), jnp.float32),
            pltpu.SemaphoreType.DMA((4,)),
        ],
        compiler_params=pltpu.CompilerParams(vmem_limit_bytes=VMEM_LIMIT),
        cost_estimate=pl.CostEstimate(flops=0, bytes_accessed=4_000_000, transcendentals=0),
    )(fine, coarse_old, arrived)


def exchange(odd, even):
    route = []
    for turn in range(T):
        for space in range(S):
            if space in (0, S - 1):
                target = (turn ^ 1) * S + space
            else:
                target = turn * S + space + 2 * (space % 2) - 1
            route.append((turn * S + space, target))
    even_route = [(i, i + 1 - 2 * (i % 2)) for i in range(S)]
    return lax.ppermute(odd, ("tm", "space"), route), lax.ppermute(even, "space", even_route)


def local(iterate, fine_prev, mobility, pending):
    tile = (HALF, CX, 128)
    early = (EARLY_TILES, CX, 128)
    late = (LATE_TILES, CX, 128)
    fields = [field.reshape(ROWS, Y) for field in (iterate, mobility, fine_prev)]
    own_odd, own_even = pack_fine(iterate[0], mobility)
    odd, even = exchange(own_odd, own_even)
    stepped, old_part, mob_tile, outer, flag = call(
        before_body, [(ROWS, Y), (CROWS, CY), tile, (2, Z, Y), (8, 128)], [(Y // 256, ROWS, 128)]
    )(pending.reshape(1, T), fields[0], fields[1])
    fine_part, sent = call(second_body, [(ROWS, Y), (T,) + tile], [(Y // 256, ROWS, 128)])(
        flag, stepped, fields[1], old_part, fields[2]
    )
    sent, change, old_change = call(
        edge_body,
        [(T,) + tile, (2, 2, Z, Y), (2, Z, CY)],
        [(2, 5, Z, Y), (2, T, HALF, 128)],
    )(flag, own_odd, own_even, odd, even, outer, sent)
    terms = lax.all_to_all(sent, "tm", 0, 0)
    odd, even, late_odd, late_even = call(pack_chain_body, [early, early, late, late])(
        terms, mob_tile
    )
    odd, even = exchange(odd, even)
    late_odd, late_even = exchange(late_odd, late_even)
    fine, coarse_old = call(repair_body, [(ROWS, Y), (CROWS, CY)])(
        fine_part, change, old_part, old_change
    )
    odd, even, fine, coarse_old = lax.optimization_barrier((odd, even, fine, coarse_old))
    part = (4, CX, 128)
    first, middle = call(chain_one_body, [(FIRST + 1,) + part, tile], [early, early])(
        terms, mob_tile, odd, even
    )
    mid_odd, mid_even = exchange(middle, middle)
    (back,) = call(chain_two_body, [(T,) + part], [early, early, late, late, tile, tile])(
        terms, mob_tile, odd, even, late_odd, late_even, first, middle, mid_odd, mid_even
    )
    arrived = lax.all_to_all(back, "tm", 0, 0)
    return finish(fine, coarse_old, arrived).reshape(1, Z, X, Y)


def solution(mesh):
    placed = (
        P("tm", None, "space", None),
        P("tm", None, "space", None),
        P(None, "space", None),
        P(),
    )
    return jax.shard_map(
        local, mesh=mesh, in_specs=placed, out_specs=P("tm", None, "space", None), check_vma=False
    )
```

time: 415 us -> 52.3 us (0.13)
  the two profiles are of different devices: /device:TPU:105 before, /device:TPU:97 now
where the time goes in v1:
time: 52.3 us; the launch traced here: 52 us
  blocking collectives  28.8 us (55%)
  starting transfers between devices  10.9 us (21%)
  Pallas kernels  8.56 us (16%)
  waiting for transfers between devices  3.01 us (6%)
  local copies, waits for them, and re-layouts  0.66 us (1%)
    all_to_all x1, blocking collectives, local(): terms = lax.all_to_all(sent, 'tm', 0, 0)  16.7 us
    all_to_all x1, blocking collectives, local(): arrived = lax.all_to_all(back, 'tm', 0, 0)  12.1 us
    ppermute x4, starting transfers between devices, exchange(): lax.ppermute(odd, ('tm', 'space'), route)  10.9 us
    ppermute x4, waiting for transfers between devices, exchange(): lax.ppermute(odd, ('tm', 'space'), route)  3 us
    pallas_call x1, Pallas kernels, local(): call(before_body, [(ROWS, Y), (CROWS, CY), tile, (2, Z, Y), (8, 128)], [(...  1.65 us
    pallas_call x1, Pallas kernels, local(): call(second_body, [(ROWS, Y), (T,) + tile], [(Y // 256, ROWS, 128)])  1.52 us
    pallas_call x1, Pallas kernels, finish(): pl.pallas_call(finish_body, out_shape=jax.ShapeDtypeStruct((ROWS, Y), jnp...  1.3 us
    pallas_call x1, Pallas kernels, pack_fine(): pl.pallas_call(pack_fine_body, out_shape=[rows, rows], in_specs=[pl.Block...  1.26 us
  transfers between devices with their start and end apart: 8, of which 2 were waited for; matrix products, arithmetic and copies ran while one was open for 0% of the time, Pallas kernels for 8%

profile of v1, /device:TPU:97, one launch (start us, length us, event | category | flops | bytes accessed | tf_op | source)
XLA Modules:
  0.0 52.0 jit_solution(10100524385703671482)
XLA Ops:
  0.0 0.0 copy-start
  0.0 0.0 copy-start.1
  0.0 1.3 %shard_map.47 = (f32[3,16,1024]{2,1,0:T(8,128)S(1)}, f32[3,16,1024]{2,1,0:T(8,128)S(1)}) custom-call(f32[16,16,1024]{2,1,0:T(8,128)} %bitcast.8, f32[16,16,1024]{2,1,0:T(8,128)} %mobility.1), custom_call_target="tpu_custom_call" | custom-call | bytes 400000 | tf_op jit(solution)/shard_map/pallas_call | solution.py:550
  1.3 3.5 %collective-permute-start = (f32[3,16,1024]{2,1,0:T(8,128)S(1)}, f32[3,16,1024]{2,1,0:T(8,128)S(1)}, u32[]{:S(2)}, u32[]{:S(2)}) collective-permute-start(f32[3,16,1024]{2,1,0:T(8,128)S(1)} %get-tuple-element.30.own_odd), channel_id=1, source_target_pairs={{0,16},{1,2},{2,1},{3,4},{4,3},{5,6},{6,5},{7,8},{8,7},{9,10},{10,... | collective-permute-start | bytes 589832 | tf_op jit(solution)/shard_map/ppermute | solution.py:587
  4.8 0.0 collective-permute-start.1
  4.8 0.0 copy-start.3
  4.8 0.0 copy-done
  4.8 0.0 copy-done.1
  4.8 0.6 %copy-done.3 = s32[16]{0:T(128)S(1)} copy-done((s32[16]{0:T(128)S(1)}, s32[16]{0:T(128)}, u32[]{:S(2)}) %copy-start.3) | copy-done | bytes 88
  5.4 0.0 copy-start.2
  5.4 1.7 %shard_map.46 = (f32[256,1024]{1,0:T(8,128)S(1)}, f32[128,512]{1,0:T(8,128)S(1)}, f32[8,8,128]{2,1,0:T(8,128)S(1)}, f32[2,16,1024]{2,1,0:T(8,128)S(1)}, f32[8,128]{1,0:T(8,128)S(1)}) custom-call(s32[1,16]{1,0:T(1,128)S(1)} %bitcast.11, f32[256,1024]{1,0:T(8,128)S(1)} %bitcast.9, f32[256,1024]{1,0:T(8,128)S(1)} %bitcast.6), custom_call_target="tpu_custom_call" | custom-call | bytes 4000000 | tf_op jit(solution)/shard_map/pallas_call | solution.py:597
  7.1 0.0 copy-done.2
  7.1 1.5 %shard_map.48 = (f32[256,1024]{1,0:T(8,128)S(1)}, f32[16,8,8,128]{3,2,1,0:T(8,128)S(1)}) custom-call(f32[8,128]{1,0:T(8,128)S(1)} %get-tuple-element.29.flag, f32[256,1024]{1,0:T(8,128)S(1)} %get-tuple-element.33.stepped, f32[256,1024]{1,0:T(8,128)S(1)} %bitcast.7, f32[128,512]{1,0:T(8,128)S(1)} %get-tuple-element.34.coarse_old.old_in, f32[256,1024]{1,0:T(8,128)S(1)} %bitcast.10), custom_call_target="tpu_custom_call" | custom-call | bytes 4000000 | tf_op jit(solution)/shard_map/pallas_call | solution.py:600
  8.6 0.0 collective-permute-done.odd
  8.6 0.0 collective-permute-done.1.even
  8.6 0.6 %shard_map.49 = (f32[16,8,8,128]{3,2,1,0:T(8,128)S(1)}, f32[2,2,16,1024]{3,2,1,0:T(8,128)S(1)}, f32[2,16,512]{2,1,0:T(8,128)S(1)}) custom-call(f32[8,128]{1,0:T(8,128)S(1)} %get-tuple-element.29.flag, f32[3,16,1024]{2,1,0:T(8,128)S(1)} %get-tuple-element.30.own_odd, f32[3,16,1024]{2,1,0:T(8,128)S(1)} %get-tuple-element.31.own_even, ...), custom_call_target="tpu_custom_call" | custom-call | bytes 4000000 | tf_op jit(solution)/shard_map/pallas_call | solution.py:603
  9.3 16.7 %all_to_all.10.terms = f32[16,8,8,128]{3,2,1,0:T(8,128)S(1)} all-to-all(f32[16,8,8,128]{3,2,1,0:T(8,128)S(1)} %get-tuple-element.36), channel_id=1, replica_groups=mesh['tm'=16,'space'=16] {'tm'}, dimensions={0} | all-to-all | bytes 1048576 | tf_op jit(solution)/shard_map/all_to_all | solution.py:608
  26.0 0.1 shard_map.50
  26.0 3.3 %collective-permute-start.2 = (f32[34,8,128]{2,1,0:T(8,128)S(1)}, f32[34,8,128]{2,1,0:T(8,128)S(1)}, u32[]{:S(2)}, u32[]{:S(2)}) collective-permute-start(f32[34,8,128]{2,1,0:T(8,128)S(1)} %get-tuple-element.38), channel_id=1, source_target_pairs={{0,16},{1,2},{2,1},{3,4},{4,3},{5,6},{6,5},{7,8},{8,7},{9,10},{10,... | collective-permute-start | bytes 417800 | tf_op jit(solution)/shard_map/ppermute | solution.py:587
  29.3 0.0 collective-permute-start.3
  29.4 1.1 %collective-permute-start.4 = (f32[32,8,128]{2,1,0:T(8,128)S(1)}, f32[32,8,128]{2,1,0:T(8,128)S(1)}, u32[]{:S(2)}, u32[]{:S(2)}) collective-permute-start(f32[32,8,128]{2,1,0:T(8,128)S(1)} %get-tuple-element.49), channel_id=1, source_target_pairs={{0,16},{1,2},{2,1},{3,4},{4,3},{5,6},{6,5},{7,8},{8,7},{9,10},{10,... | collective-permute-start | bytes 393224 | tf_op jit(solution)/shard_map/ppermute | solution.py:587
  30.4 0.0 collective-permute-start.5
  30.4 0.3 shard_map.51
  30.7 1.4 %collective-permute-done.2.odd = f32[34,8,128]{2,1,0:T(8,128)S(1)} collective-permute-done((f32[34,8,128]{2,1,0:T(8,128)S(1)}, f32[34,8,128]{2,1,0:T(8,128)S(1)}, u32[]{:S(2)}, u32[]{:S(2)}) %collective-permute-start.2) | collective-permute-done | bytes 139296 | tf_op jit(solution)/shard_map/ppermute | solution.py:587
  32.1 0.0 collective-permute-done.3.even
  32.1 0.9 %shard_map.52 = (f32[8,4,8,128]{3,2,1,0:T(8,128)S(1)}, f32[8,8,128]{2,1,0:T(8,128)S(1)}) custom-call(f32[16,8,8,128]{3,2,1,0:T(8,128)S(1)} %all_to_all.10.terms, f32[8,8,128]{2,1,0:T(8,128)S(1)} %get-tuple-element.37.mob_tile, f32[34,8,128]{2,1,0:T(8,128)S(1)} %collective-permute-done.2.odd, f32[34,8,128]{2,1,0:T(8,128)S(1)} %collective-permute-done.3.even), custom_call_target="tpu_custom_call" | custom-call | bytes 4000000 | tf_op jit(solution)/shard_map/pallas_call | solution.py:619
  33.0 3.0 %collective-permute-start.6 = (f32[8,8,128]{2,1,0:T(8,128)S(1)}, f32[8,8,128]{2,1,0:T(8,128)S(1)}, u32[]{:S(2)}, u32[]{:S(2)}) collective-permute-start(f32[8,8,128]{2,1,0:T(8,128)S(1)} %get-tuple-element.52.middle), channel_id=1, source_target_pairs={{0,16},{1,2},{2,1},{3,4},{4,3},{5,6},{6,5},{7,8},{8,7},{9,10},{10,... | collective-permute-start | bytes 98312 | tf_op jit(solution)/shard_map/ppermute | solution.py:587
  36.0 0.0 collective-permute-start.7
  36.0 0.0 collective-permute-done.4.late_odd
  36.0 0.0 collective-permute-done.5.late_even
  36.0 1.6 %collective-permute-done.6.mid_odd = f32[8,8,128]{2,1,0:T(8,128)S(1)} collective-permute-done((f32[8,8,128]{2,1,0:T(8,128)S(1)}, f32[8,8,128]{2,1,0:T(8,128)S(1)}, u32[]{:S(2)}, u32[]{:S(2)}) %collective-permute-start.6) | collective-permute-done | bytes 32800 | tf_op jit(solution)/shard_map/ppermute | solution.py:587
  37.6 0.0 collective-permute-done.7.mid_even
  37.6 1.0 %shard_map.53 = f32[16,4,8,128]{3,2,1,0:T(8,128)S(1)} custom-call(f32[16,8,8,128]{3,2,1,0:T(8,128)S(1)} %all_to_all.10.terms, f32[8,8,128]{2,1,0:T(8,128)S(1)} %get-tuple-element.37.mob_tile, f32[34,8,128]{2,1,0:T(8,128)S(1)} %collective-permute-done.2.odd, f32[34,8,128]{2,1,0:T(8,128)S(1)} %collective-permute-done.3.even, ...), custom_call_target="tpu_custom_call" | custom-call | bytes 4000000 | tf_op jit(solution)/shard_map/pallas_call | solution.py:623
  38.6 12.1 %all_to_all.11.arrived = f32[16,4,8,128]{3,2,1,0:T(8,128)S(1)} all-to-all(f32[16,4,8,128]{3,2,1,0:T(8,128)S(1)} %shard_map.53), channel_id=1, replica_groups=mesh['tm'=16,'space'=16] {'tm'}, dimensions={0} | all-to-all | bytes 524288 | tf_op jit(solution)/shard_map/all_to_all | solution.py:626
  50.7 1.3 %shard_map.54 = f32[256,1024]{1,0:T(8,128)} custom-call(f32[256,1024]{1,0:T(8,128)S(1)} %get-tuple-element.45.fine, f32[128,512]{1,0:T(8,128)S(1)} %get-tuple-element.46.coarse_old, f32[16,4,8,128]{3,2,1,0:T(8,128)S(1)} %all_to_all.11.arrived), custom_call_target="tpu_custom_call" | custom-call | bytes 4000000 | tf_op jit(solution)/shard_map/pallas_call | solution.py:562
Async XLA Ops:
  0.0 4.8 %copy-start = (f32[16,16,1024]{2,1,0:T(8,128)S(1)}, f32[16,16,1024]{2,1,0:T(8,128)}, u32[]{:S(2)}) copy-start(f32[16,16,1024]{2,1,0:T(8,128)} %mobility.1) | copy-start | bytes 3145732
  0.0 4.8 %copy-start.1 = (f32[1,16,16,1024]{3,2,1,0:T(8,128)S(1)}, f32[1,16,16,1024]{3,2,1,0:T(8,128)}, u32[]{:S(2)}) copy-start(f32[1,16,16,1024]{3,2,1,0:T(8,128)} %param.4) | copy-start | bytes 3145732
  1.3 7.4 %collective-permute-start = (f32[3,16,1024]{2,1,0:T(8,128)S(1)}, f32[3,16,1024]{2,1,0:T(8,128)S(1)}, u32[]{:S(2)}, u32[]{:S(2)}) collective-permute-start(f32[3,16,1024]{2,1,0:T(8,128)S(1)} %get-tuple-element.30.own_odd), channel_id=1, source_target_pairs={{0,16},{1,2},{2,1},{3,4},{4,3},{5,6},{6,5},{7,8},{8,7},{9,10},{10,... | collective-permute-start | bytes 589832 | tf_op jit(solution)/shard_map/ppermute | solution.py:587
  4.8 3.9 %collective-permute-start.1 = (f32[3,16,1024]{2,1,0:T(8,128)S(1)}, f32[3,16,1024]{2,1,0:T(8,128)S(1)}, u32[]{:S(2)}, u32[]{:S(2)}) collective-permute-start(f32[3,16,1024]{2,1,0:T(8,128)S(1)} %get-tuple-element.31.own_even), channel_id=1, source_target_pairs={{0,1},{1,0},{2,3},{3,2},{4,5},{5,4},{6,7},{7,6},{8,9},{9,8},{10,11... | collective-permute-start | bytes 589832 | tf_op jit(solution)/shard_map/ppermute | solution.py:587
  4.8 0.7 %copy-start.3 = (s32[16]{0:T(128)S(1)}, s32[16]{0:T(128)}, u32[]{:S(2)}) copy-start(s32[16]{0:T(128)} %param.7) | copy-start | bytes 196
  5.4 1.7 %copy-start.2 = (f32[1,16,16,1024]{3,2,1,0:T(8,128)S(1)}, f32[1,16,16,1024]{3,2,1,0:T(8,128)}, u32[]{:S(2)}) copy-start(f32[1,16,16,1024]{3,2,1,0:T(8,128)} %param.5) | copy-start | bytes 3145732
  26.0 6.1 %collective-permute-start.2 = (f32[34,8,128]{2,1,0:T(8,128)S(1)}, f32[34,8,128]{2,1,0:T(8,128)S(1)}, u32[]{:S(2)}, u32[]{:S(2)}) collective-permute-start(f32[34,8,128]{2,1,0:T(8,128)S(1)} %get-tuple-element.38), channel_id=1, source_target_pairs={{0,16},{1,2},{2,1},{3,4},{4,3},{5,6},{6,5},{7,8},{8,7},{9,10},{10,... | collective-permute-start | bytes 417800 | tf_op jit(solution)/shard_map/ppermute | solution.py:587
  29.3 2.7 %collective-permute-start.3 = (f32[34,8,128]{2,1,0:T(8,128)S(1)}, f32[34,8,128]{2,1,0:T(8,128)S(1)}, u32[]{:S(2)}, u32[]{:S(2)}) collective-permute-start(f32[34,8,128]{2,1,0:T(8,128)S(1)} %get-tuple-element.39), channel_id=1, source_target_pairs={{0,1},{1,0},{2,3},{3,2},{4,5},{5,4},{6,7},{7,6},{8,9},{9,8},{10,11... | collective-permute-start | bytes 417800 | tf_op jit(solution)/shard_map/ppermute | solution.py:587
  29.4 6.6 %collective-permute-start.4 = (f32[32,8,128]{2,1,0:T(8,128)S(1)}, f32[32,8,128]{2,1,0:T(8,128)S(1)}, u32[]{:S(2)}, u32[]{:S(2)}) collective-permute-start(f32[32,8,128]{2,1,0:T(8,128)S(1)} %get-tuple-element.49), channel_id=1, source_target_pairs={{0,16},{1,2},{2,1},{3,4},{4,3},{5,6},{6,5},{7,8},{8,7},{9,10},{10,... | collective-permute-start | bytes 393224 | tf_op jit(solution)/shard_map/ppermute | solution.py:587
  30.4 5.6 %collective-permute-start.5 = (f32[32,8,128]{2,1,0:T(8,128)S(1)}, f32[32,8,128]{2,1,0:T(8,128)S(1)}, u32[]{:S(2)}, u32[]{:S(2)}) collective-permute-start(f32[32,8,128]{2,1,0:T(8,128)S(1)} %get-tuple-element.50), channel_id=1, source_target_pairs={{0,1},{1,0},{2,3},{3,2},{4,5},{5,4},{6,7},{7,6},{8,9},{9,8},{10,11... | collective-permute-start | bytes 393224 | tf_op jit(solution)/shard_map/ppermute | solution.py:587
  33.0 4.6 %collective-permute-start.6 = (f32[8,8,128]{2,1,0:T(8,128)S(1)}, f32[8,8,128]{2,1,0:T(8,128)S(1)}, u32[]{:S(2)}, u32[]{:S(2)}) collective-permute-start(f32[8,8,128]{2,1,0:T(8,128)S(1)} %get-tuple-element.52.middle), channel_id=1, source_target_pairs={{0,16},{1,2},{2,1},{3,4},{4,3},{5,6},{6,5},{7,8},{8,7},{9,10},{10,... | collective-permute-start | bytes 98312 | tf_op jit(solution)/shard_map/ppermute | solution.py:587
  36.0 1.6 %collective-permute-start.7 = (f32[8,8,128]{2,1,0:T(8,128)S(1)}, f32[8,8,128]{2,1,0:T(8,128)S(1)}, u32[]{:S(2)}, u32[]{:S(2)}) collective-permute-start(f32[8,8,128]{2,1,0:T(8,128)S(1)} %get-tuple-element.52.middle), channel_id=1, source_target_pairs={{0,1},{1,0},{2,3},{3,2},{4,5},{5,4},{6,7},{7,6},{8,9},{9,8},{10,11... | collective-permute-start | bytes 98312 | tf_op jit(solution)/shard_map/ppermute | solution.py:587

commit v2 on v1

--- a/solution.py
+++ b/solution.py
@@ -17,6 +17,7 @@
 OWN = CY // T
 MARGIN = 16
 HALF = Z // 2
+PACKED = 2 * Z + HALF
 FIRST = 7
 SPAN = 3 * CX
 
@@ -126,20 +127,34 @@
     return fine_rule(center, around, mob_ref[pl.ds(base, 8), :])
 
 
-def pack_fine_body(iterate, mobility, odd, even, done):
+def pack_fine_body(iterate, mobility, odd, even, own_mob, rows, done):
     space = lax.axis_index("space")
+    ends = ((0, 1), (X - 1, X - 2))
+    moves = []
+    for side, (near, far) in enumerate(ends):
+        for source, inner, target in (
+            (iterate, near, rows.at[side, 0]),
+            (iterate, far, rows.at[side, 1]),
+            (mobility, near, own_mob.at[side]),
+        ):
+            moves.append(
+                pltpu.make_async_copy(source.at[:, inner, :], target, done.at[len(moves)])
+            )
+    for move in moves:
+        move.start()
+    for move in moves:
+        move.wait()
+    sums = [rows[side, 0] + rows[side, 1] for side in range(2)]
+    halved = halve_lanes(jnp.concatenate(sums, axis=0))
 
     def put(low, high):
-        moves = []
-        for out, near, far in ((low, 0, 1), (high, X - 1, X - 2)):
-            for k, (source, inner) in enumerate(((iterate, near), (iterate, far), (mobility, near))):
-                moves.append(
-                    pltpu.make_async_copy(source.at[:, inner, :], out.at[k], done.at[len(moves)])
-                )
-        for move in moves:
-            move.start()
-        for move in moves:
-            move.wait()
+        for side, out in enumerate((low, high)):
+            near, far = rows[side, 0], rows[side, 1]
+            out[pl.ds(0, Z), :] = near
+            out[pl.ds(Z, Z), :] = fine_rule(near, far, own_mob[side])
+            coarse = halved[side * Z : (side + 1) * Z]
+            out[pl.ds(2 * Z, HALF), pl.ds(0, CY)] = coarse[:HALF]
+            out[pl.ds(2 * Z, HALF), pl.ds(CY, CY)] = coarse[HALF:]
 
     pl.when(space % 2 == 0)(lambda: put(odd, even))
     pl.when(space % 2 == 1)(lambda: put(even, odd))
@@ -274,17 +289,16 @@
 
 
 def edge_body(
-    flag, own_odd, own_even, odd, even, outer, sent_in, sent, change, old_change, halo, added_rows
+    flag, own_odd, own_even, odd, even, own_mob, outer, sent_in,
+    sent, change, old_change, halo, added_rows,
 ):
     space = lax.axis_index("space")
     turn = lax.axis_index("tm")
 
     def take(low, high, own_low, own_high):
         for side, (got, own) in enumerate(((low, own_low), (high, own_high))):
-            for k in range(3):
-                halo[side, k] = got[k]
-            halo[side, 3] = own[0]
-            halo[side, 4] = own[2]
+            halo[side, pl.ds(0, PACKED), :] = got[...]
+            halo[side, pl.ds(PACKED, Z), :] = own[pl.ds(0, Z), :]
 
     pl.when(space % 2 == 0)(lambda: take(odd, even, own_odd, own_even))
     pl.when(space % 2 == 1)(lambda: take(even, odd, own_even, own_odd))
@@ -298,27 +312,29 @@
         total += jnp.where(plane == Z - 1, 0.0, pltpu.roll(value, Z - 1, 0))
         return total + beside_lanes(value)
 
-    sums = [None] * 4
+    sums, coarse_sides = [], []
     for side, inside in ((0, space > 0), (1, space < S - 1)):
         keep = jnp.where(inside, 1.0, 0.0)
-        near, far, mob = keep * halo[side, 0], keep * halo[side, 1], halo[side, 2]
-        own, own_mob = halo[side, 3], halo[side, 4]
-        beyond = keep * fine_rule(near, far + own + beside(near), mob)
+        near, given = keep * halo[side, pl.ds(0, Z), :], halo[side, pl.ds(Z, Z), :]
+        own, own_mobility = halo[side, pl.ds(PACKED, Z), :], own_mob[side]
+        beyond = keep * (given + DIFFUSE * (own + beside(near)))
+        planes = pl.ds(2 * Z, HALF)
+        coarse = [halo[side, planes, pl.ds(half * CY, CY)] for half in range(2)]
+        coarse_sides.append((keep * 0.5 * DIFFUSE * 0.25) * jnp.concatenate(coarse, axis=0))
         added = DIFFUSE * near
         before = outer[side]
         after = before + added
         grown = after * (1.0 - after * after) - before * (1.0 - before * before)
         first = added + DIFFUSE * (beyond + beside(added) - 6.0 * added)
-        first = flagged * (first + REACTION * own_mob * grown)
+        first = flagged * (first + REACTION * own_mobility * grown)
         second = flagged * DIFFUSE * added
         change[side, 0] = first
         change[side, 1] = second
-        sums[side] = near + far
-        sums[2 + side] = first + second
+        sums.append(first + second)
     halved = halve_lanes(jnp.concatenate(sums, axis=0))
     for side in range(2):
-        coarse_side = (0.5 * DIFFUSE * 0.25) * halved[side * Z : (side + 1) * Z]
-        fine_side = 0.25 * halved[(2 + side) * Z : (3 + side) * Z]
+        coarse_side = coarse_sides[side]
+        fine_side = 0.25 * halved[side * Z : (side + 1) * Z]
         old_change[side] = coarse_side
         for tile, value in enumerate(edge_windows(fine_side - weight * coarse_side)):
             added_rows[side, tile] = value
@@ -546,13 +562,13 @@
 
 
 def pack_fine(iterate, mobility):
-    rows = jax.ShapeDtypeStruct((3, Z, Y), jnp.float32)
+    outs = [(PACKED, Y), (PACKED, Y), (2, Z, Y)]
     return pl.pallas_call(
         pack_fine_body,
-        out_shape=[rows, rows],
+        out_shape=[jax.ShapeDtypeStruct(shape, jnp.float32) for shape in outs],
         in_specs=[pl.BlockSpec(memory_space=pltpu.HBM)] * 2,
-        out_specs=[pl.BlockSpec(memory_space=pltpu.VMEM)] * 2,
-        scratch_shapes=[pltpu.SemaphoreType.DMA((6,))],
+        out_specs=[pl.BlockSpec(memory_space=pltpu.VMEM)] * 3,
+        scratch_shapes=[pltpu.VMEM((2, 2, Z, Y), jnp.float32), pltpu.SemaphoreType.DMA((6,))],
         compiler_params=pltpu.CompilerParams(vmem_limit_bytes=PACK_VMEM),
         cost_estimate=pl.CostEstimate(flops=0, bytes_accessed=400_000, transcendentals=0),
     )(iterate, mobility)
@@ -592,7 +608,7 @@
     early = (EARLY_TILES, CX, 128)
     late = (LATE_TILES, CX, 128)
     fields = [field.reshape(ROWS, Y) for field in (iterate, mobility, fine_prev)]
-    own_odd, own_even = pack_fine(iterate[0], mobility)
+    own_odd, own_even, own_mob = pack_fine(iterate[0], mobility)
     odd, even = exchange(own_odd, own_even)
     stepped, old_part, mob_tile, outer, flag = call(
         before_body, [(ROWS, Y), (CROWS, CY), tile, (2, Z, Y), (8, 128)], [(Y // 256, ROWS, 128)]
@@ -603,8 +619,8 @@
     sent, change, old_change = call(
         edge_body,
         [(T,) + tile, (2, 2, Z, Y), (2, Z, CY)],
-        [(2, 5, Z, Y), (2, T, HALF, 128)],
-    )(flag, own_odd, own_even, odd, even, outer, sent)
+        [(2, PACKED + Z, Y), (2, T, HALF, 128)],
+    )(flag, own_odd, own_even, odd, even, own_mob, outer, sent)
     terms = lax.all_to_all(sent, "tm", 0, 0)
     odd, even, late_odd, late_even = call(pack_chain_body, [early, early, late, late])(
         terms, mob_tile

time: 52.3 us -> 52 us (level)
  starting transfers between devices: 10.9 us -> 10.1 us
  blocking collectives: 28.8 us -> 29.4 us
    all_to_all x1, blocking collectives: 16.7 us -> 17.6 us  [local(): terms = lax.all_to_all(sent, 'tm', 0, 0)]
    ppermute x4, starting transfers between devices: 10.9 us -> 10.1 us  [exchange(): lax.ppermute(odd, ('tm', 'space'), route)]
    pallas_call x1, Pallas kernels: 1.52 us -> 0.8 us  [local(): call(second_body, [(ROWS, Y), (T,) + tile], [(Y // 256, ROWS, 128)])]
  transfers between devices with their start and end apart: 8 -> 8, of which waited for: 2 -> 2; matrix products, arithmetic and copies ran while one was open for 0% -> 0% of each run, Pallas kernels for 8% -> 7%
where the time goes in v2:
time: 52 us; the launch traced here: 51.8 us
  blocking collectives  29.4 us (57%)
  starting transfers between devices  10.1 us (19%)
  Pallas kernels  8.04 us (15%)
  waiting for transfers between devices  3.48 us (7%)
  local copies, waits for them, and re-layouts  0.66 us (1%)
    all_to_all x1, blocking collectives, local(): terms = lax.all_to_all(sent, 'tm', 0, 0)  17.6 us
    all_to_all x1, blocking collectives, local(): arrived = lax.all_to_all(back, 'tm', 0, 0)  11.9 us
    ppermute x4, starting transfers between devices, exchange(): lax.ppermute(odd, ('tm', 'space'), route)  10.1 us
    ppermute x4, waiting for transfers between devices, exchange(): lax.ppermute(odd, ('tm', 'space'), route)  3.47 us
    pallas_call x1, Pallas kernels, local(): call(before_body, [(ROWS, Y), (CROWS, CY), tile, (2, Z, Y), (8, 128)], [(...  1.65 us
    pallas_call x1, Pallas kernels, pack_fine(): pl.pallas_call(pack_fine_body, out_shape=[jax.ShapeDtypeStruct(shape, jnp...  1.51 us
    pallas_call x1, Pallas kernels, finish(): pl.pallas_call(finish_body, out_shape=jax.ShapeDtypeStruct((ROWS, Y), jnp...  1.3 us
  transfers between devices with their start and end apart: 8, of which 2 were waited for; matrix products, arithmetic and copies ran while one was open for 0% of the time, Pallas kernels for 7%

profile of v2, /device:TPU:97, one launch (start us, length us, event | category | flops | bytes accessed | tf_op | source)
XLA Modules:
  0.0 51.8 jit_solution(16439342294323086154)
XLA Ops:
  0.0 0.0 copy-start
  0.0 0.0 copy-start.1
  0.0 1.5 %shard_map.47 = (f32[40,1024]{1,0:T(8,128)S(1)}, f32[40,1024]{1,0:T(8,128)S(1)}, f32[2,16,1024]{2,1,0:T(8,128)S(1)}) custom-call(f32[16,16,1024]{2,1,0:T(8,128)} %bitcast.8, f32[16,16,1024]{2,1,0:T(8,128)} %mobility.1), custom_call_target="tpu_custom_call" | custom-call | bytes 400000 | tf_op jit(solution)/shard_map/pallas_call | solution.py:566
  1.5 3.5 %collective-permute-start = (f32[40,1024]{1,0:T(8,128)S(1)}, f32[40,1024]{1,0:T(8,128)S(1)}, u32[]{:S(2)}, u32[]{:S(2)}) collective-permute-start(f32[40,1024]{1,0:T(8,128)S(1)} %get-tuple-element.31.own_odd), channel_id=1, source_target_pairs={{0,16},{1,2},{2,1},{3,4},{4,3},{5,6},{6,5},{7,8},{8,7},{9,10},{10,... | collective-permute-start | bytes 491528 | tf_op jit(solution)/shard_map/ppermute | solution.py:603
  5.0 0.0 collective-permute-start.1
  5.0 0.0 copy-start.3
  5.0 0.0 copy-done
  5.0 0.0 copy-done.1
  5.0 0.6 %copy-done.3 = s32[16]{0:T(128)S(1)} copy-done((s32[16]{0:T(128)S(1)}, s32[16]{0:T(128)}, u32[]{:S(2)}) %copy-start.3) | copy-done | bytes 88
  5.7 0.0 copy-start.2
  5.7 1.6 %shard_map.46 = (f32[256,1024]{1,0:T(8,128)S(1)}, f32[128,512]{1,0:T(8,128)S(1)}, f32[8,8,128]{2,1,0:T(8,128)S(1)}, f32[2,16,1024]{2,1,0:T(8,128)S(1)}, f32[8,128]{1,0:T(8,128)S(1)}) custom-call(s32[1,16]{1,0:T(1,128)S(1)} %bitcast.11, f32[256,1024]{1,0:T(8,128)S(1)} %bitcast.9, f32[256,1024]{1,0:T(8,128)S(1)} %bitcast.6), custom_call_target="tpu_custom_call" | custom-call | bytes 4000000 | tf_op jit(solution)/shard_map/pallas_call | solution.py:613
  7.3 0.0 copy-done.2
  7.3 0.8 %shard_map.48 = (f32[256,1024]{1,0:T(8,128)S(1)}, f32[16,8,8,128]{3,2,1,0:T(8,128)S(1)}) custom-call(f32[8,128]{1,0:T(8,128)S(1)} %get-tuple-element.30.flag, f32[256,1024]{1,0:T(8,128)S(1)} %get-tuple-element.35.stepped, f32[256,1024]{1,0:T(8,128)S(1)} %bitcast.7, f32[128,512]{1,0:T(8,128)S(1)} %get-tuple-element.36.coarse_old.old_in, f32[256,1024]{1,0:T(8,128)S(1)} %bitcast.10), custom_call_target="tpu_custom_call" | custom-call | bytes 4000000 | tf_op jit(solution)/shard_map/pallas_call | solution.py:616
  8.1 0.0 collective-permute-done.odd
  8.2 0.0 collective-permute-done.1.even
  8.2 0.6 %shard_map.49 = (f32[16,8,8,128]{3,2,1,0:T(8,128)S(1)}, f32[2,2,16,1024]{3,2,1,0:T(8,128)S(1)}, f32[2,16,512]{2,1,0:T(8,128)S(1)}) custom-call(f32[8,128]{1,0:T(8,128)S(1)} %get-tuple-element.30.flag, f32[40,1024]{1,0:T(8,128)S(1)} %get-tuple-element.31.own_odd, f32[40,1024]{1,0:T(8,128)S(1)} %get-tuple-element.32.own_even, ...), custom_call_target="tpu_custom_call" | custom-call | bytes 4000000 | tf_op jit(solution)/shard_map/pallas_call | solution.py:619
  8.8 17.6 %all_to_all.10.terms = f32[16,8,8,128]{3,2,1,0:T(8,128)S(1)} all-to-all(f32[16,8,8,128]{3,2,1,0:T(8,128)S(1)} %get-tuple-element.38), channel_id=1, replica_groups=mesh['tm'=16,'space'=16] {'tm'}, dimensions={0} | all-to-all | bytes 1048576 | tf_op jit(solution)/shard_map/all_to_all | solution.py:624
  26.3 0.1 shard_map.50
  26.4 2.8 %collective-permute-start.2 = (f32[34,8,128]{2,1,0:T(8,128)S(1)}, f32[34,8,128]{2,1,0:T(8,128)S(1)}, u32[]{:S(2)}, u32[]{:S(2)}) collective-permute-start(f32[34,8,128]{2,1,0:T(8,128)S(1)} %get-tuple-element.40), channel_id=1, source_target_pairs={{0,16},{1,2},{2,1},{3,4},{4,3},{5,6},{6,5},{7,8},{8,7},{9,10},{10,... | collective-permute-start | bytes 417800 | tf_op jit(solution)/shard_map/ppermute | solution.py:603
  29.2 0.0 collective-permute-start.3
  29.2 1.1 %collective-permute-start.4 = (f32[32,8,128]{2,1,0:T(8,128)S(1)}, f32[32,8,128]{2,1,0:T(8,128)S(1)}, u32[]{:S(2)}, u32[]{:S(2)}) collective-permute-start(f32[32,8,128]{2,1,0:T(8,128)S(1)} %get-tuple-element.51), channel_id=1, source_target_pairs={{0,16},{1,2},{2,1},{3,4},{4,3},{5,6},{6,5},{7,8},{8,7},{9,10},{10,... | collective-permute-start | bytes 393224 | tf_op jit(solution)/shard_map/ppermute | solution.py:603
  30.3 0.0 collective-permute-start.5
  30.3 0.3 shard_map.51
  30.5 1.6 %collective-permute-done.2.odd = f32[34,8,128]{2,1,0:T(8,128)S(1)} collective-permute-done((f32[34,8,128]{2,1,0:T(8,128)S(1)}, f32[34,8,128]{2,1,0:T(8,128)S(1)}, u32[]{:S(2)}, u32[]{:S(2)}) %collective-permute-start.2) | collective-permute-done | bytes 139296 | tf_op jit(solution)/shard_map/ppermute | solution.py:603
  32.2 0.0 collective-permute-done.3.even
  32.2 0.9 %shard_map.52 = (f32[8,4,8,128]{3,2,1,0:T(8,128)S(1)}, f32[8,8,128]{2,1,0:T(8,128)S(1)}) custom-call(f32[16,8,8,128]{3,2,1,0:T(8,128)S(1)} %all_to_all.10.terms, f32[8,8,128]{2,1,0:T(8,128)S(1)} %get-tuple-element.39.mob_tile, f32[34,8,128]{2,1,0:T(8,128)S(1)} %collective-permute-done.2.odd, f32[34,8,128]{2,1,0:T(8,128)S(1)} %collective-permute-done.3.even), custom_call_target="tpu_custom_call" | custom-call | bytes 4000000 | tf_op jit(solution)/shard_map/pallas_call | solution.py:635
  33.0 2.8 %collective-permute-start.6 = (f32[8,8,128]{2,1,0:T(8,128)S(1)}, f32[8,8,128]{2,1,0:T(8,128)S(1)}, u32[]{:S(2)}, u32[]{:S(2)}) collective-permute-start(f32[8,8,128]{2,1,0:T(8,128)S(1)} %get-tuple-element.54.middle), channel_id=1, source_target_pairs={{0,16},{1,2},{2,1},{3,4},{4,3},{5,6},{6,5},{7,8},{8,7},{9,10},{10,... | collective-permute-start | bytes 98312 | tf_op jit(solution)/shard_map/ppermute | solution.py:603
  35.8 0.0 collective-permute-start.7
  35.8 0.0 collective-permute-done.4.late_odd
  35.8 0.0 collective-permute-done.5.late_even
  35.8 1.8 %collective-permute-done.6.mid_odd = f32[8,8,128]{2,1,0:T(8,128)S(1)} collective-permute-done((f32[8,8,128]{2,1,0:T(8,128)S(1)}, f32[8,8,128]{2,1,0:T(8,128)S(1)}, u32[]{:S(2)}, u32[]{:S(2)}) %collective-permute-start.6) | collective-permute-done | bytes 32800 | tf_op jit(solution)/shard_map/ppermute | solution.py:603
  37.7 0.0 collective-permute-done.7.mid_even
  37.7 1.0 %shard_map.53 = f32[16,4,8,128]{3,2,1,0:T(8,128)S(1)} custom-call(f32[16,8,8,128]{3,2,1,0:T(8,128)S(1)} %all_to_all.10.terms, f32[8,8,128]{2,1,0:T(8,128)S(1)} %get-tuple-element.39.mob_tile, f32[34,8,128]{2,1,0:T(8,128)S(1)} %collective-permute-done.2.odd, f32[34,8,128]{2,1,0:T(8,128)S(1)} %collective-permute-done.3.even, ...), custom_call_target="tpu_custom_call" | custom-call | bytes 4000000 | tf_op jit(solution)/shard_map/pallas_call | solution.py:639
  38.7 11.9 %all_to_all.11.arrived = f32[16,4,8,128]{3,2,1,0:T(8,128)S(1)} all-to-all(f32[16,4,8,128]{3,2,1,0:T(8,128)S(1)} %shard_map.53), channel_id=1, replica_groups=mesh['tm'=16,'space'=16] {'tm'}, dimensions={0} | all-to-all | bytes 524288 | tf_op jit(solution)/shard_map/all_to_all | solution.py:642
  50.5 1.3 %shard_map.54 = f32[256,1024]{1,0:T(8,128)} custom-call(f32[256,1024]{1,0:T(8,128)S(1)} %get-tuple-element.47.fine, f32[128,512]{1,0:T(8,128)S(1)} %get-tuple-element.48.coarse_old, f32[16,4,8,128]{3,2,1,0:T(8,128)S(1)} %all_to_all.11.arrived), custom_call_target="tpu_custom_call" | custom-call | bytes 4000000 | tf_op jit(solution)/shard_map/pallas_call | solution.py:578
Async XLA Ops:
  0.0 5.0 %copy-start = (f32[16,16,1024]{2,1,0:T(8,128)S(1)}, f32[16,16,1024]{2,1,0:T(8,128)}, u32[]{:S(2)}) copy-start(f32[16,16,1024]{2,1,0:T(8,128)} %mobility.1) | copy-start | bytes 3145732
  0.0 5.0 %copy-start.1 = (f32[1,16,16,1024]{3,2,1,0:T(8,128)S(1)}, f32[1,16,16,1024]{3,2,1,0:T(8,128)}, u32[]{:S(2)}) copy-start(f32[1,16,16,1024]{3,2,1,0:T(8,128)} %param.4) | copy-start | bytes 3145732
  1.5 6.6 %collective-permute-start = (f32[40,1024]{1,0:T(8,128)S(1)}, f32[40,1024]{1,0:T(8,128)S(1)}, u32[]{:S(2)}, u32[]{:S(2)}) collective-permute-start(f32[40,1024]{1,0:T(8,128)S(1)} %get-tuple-element.31.own_odd), channel_id=1, source_target_pairs={{0,16},{1,2},{2,1},{3,4},{4,3},{5,6},{6,5},{7,8},{8,7},{9,10},{10,... | collective-permute-start | bytes 491528 | tf_op jit(solution)/shard_map/ppermute | solution.py:603
  5.0 3.1 %collective-permute-start.1 = (f32[40,1024]{1,0:T(8,128)S(1)}, f32[40,1024]{1,0:T(8,128)S(1)}, u32[]{:S(2)}, u32[]{:S(2)}) collective-permute-start(f32[40,1024]{1,0:T(8,128)S(1)} %get-tuple-element.32.own_even), channel_id=1, source_target_pairs={{0,1},{1,0},{2,3},{3,2},{4,5},{5,4},{6,7},{7,6},{8,9},{9,8},{10,11... | collective-permute-start | bytes 491528 | tf_op jit(solution)/shard_map/ppermute | solution.py:603
  5.0 0.7 %copy-start.3 = (s32[16]{0:T(128)S(1)}, s32[16]{0:T(128)}, u32[]{:S(2)}) copy-start(s32[16]{0:T(128)} %param.7) | copy-start | bytes 196
  5.7 1.7 %copy-start.2 = (f32[1,16,16,1024]{3,2,1,0:T(8,128)S(1)}, f32[1,16,16,1024]{3,2,1,0:T(8,128)}, u32[]{:S(2)}) copy-start(f32[1,16,16,1024]{3,2,1,0:T(8,128)} %param.5) | copy-start | bytes 3145732
  26.4 5.8 %collective-permute-start.2 = (f32[34,8,128]{2,1,0:T(8,128)S(1)}, f32[34,8,128]{2,1,0:T(8,128)S(1)}, u32[]{:S(2)}, u32[]{:S(2)}) collective-permute-start(f32[34,8,128]{2,1,0:T(8,128)S(1)} %get-tuple-element.40), channel_id=1, source_target_pairs={{0,16},{1,2},{2,1},{3,4},{4,3},{5,6},{6,5},{7,8},{8,7},{9,10},{10,... | collective-permute-start | bytes 417800 | tf_op jit(solution)/shard_map/ppermute | solution.py:603
  29.2 3.0 %collective-permute-start.3 = (f32[34,8,128]{2,1,0:T(8,128)S(1)}, f32[34,8,128]{2,1,0:T(8,128)S(1)}, u32[]{:S(2)}, u32[]{:S(2)}) collective-permute-start(f32[34,8,128]{2,1,0:T(8,128)S(1)} %get-tuple-element.41), channel_id=1, source_target_pairs={{0,1},{1,0},{2,3},{3,2},{4,5},{5,4},{6,7},{7,6},{8,9},{9,8},{10,11... | collective-permute-start | bytes 417800 | tf_op jit(solution)/shard_map/ppermute | solution.py:603
  29.2 6.6 %collective-permute-start.4 = (f32[32,8,128]{2,1,0:T(8,128)S(1)}, f32[32,8,128]{2,1,0:T(8,128)S(1)}, u32[]{:S(2)}, u32[]{:S(2)}) collective-permute-start(f32[32,8,128]{2,1,0:T(8,128)S(1)} %get-tuple-element.51), channel_id=1, source_target_pairs={{0,16},{1,2},{2,1},{3,4},{4,3},{5,6},{6,5},{7,8},{8,7},{9,10},{10,... | collective-permute-start | bytes 393224 | tf_op jit(solution)/shard_map/ppermute | solution.py:603
  30.3 5.6 %collective-permute-start.5 = (f32[32,8,128]{2,1,0:T(8,128)S(1)}, f32[32,8,128]{2,1,0:T(8,128)S(1)}, u32[]{:S(2)}, u32[]{:S(2)}) collective-permute-start(f32[32,8,128]{2,1,0:T(8,128)S(1)} %get-tuple-element.52), channel_id=1, source_target_pairs={{0,1},{1,0},{2,3},{3,2},{4,5},{5,4},{6,7},{7,6},{8,9},{9,8},{10,11... | collective-permute-start | bytes 393224 | tf_op jit(solution)/shard_map/ppermute | solution.py:603
  33.0 4.6 %collective-permute-start.6 = (f32[8,8,128]{2,1,0:T(8,128)S(1)}, f32[8,8,128]{2,1,0:T(8,128)S(1)}, u32[]{:S(2)}, u32[]{:S(2)}) collective-permute-start(f32[8,8,128]{2,1,0:T(8,128)S(1)} %get-tuple-element.54.middle), channel_id=1, source_target_pairs={{0,16},{1,2},{2,1},{3,4},{4,3},{5,6},{6,5},{7,8},{8,7},{9,10},{10,... | collective-permute-start | bytes 98312 | tf_op jit(solution)/shard_map/ppermute | solution.py:603
  35.8 1.8 %collective-permute-start.7 = (f32[8,8,128]{2,1,0:T(8,128)S(1)}, f32[8,8,128]{2,1,0:T(8,128)S(1)}, u32[]{:S(2)}, u32[]{:S(2)}) collective-permute-start(f32[8,8,128]{2,1,0:T(8,128)S(1)} %get-tuple-element.54.middle), channel_id=1, source_target_pairs={{0,1},{1,0},{2,3},{3,2},{4,5},{5,4},{6,7},{7,6},{8,9},{9,8},{10,11... | collective-permute-start | bytes 98312 | tf_op jit(solution)/shard_map/ppermute | solution.py:603

commit v3 on v1

--- a/solution.py
+++ b/solution.py
@@ -274,61 +274,56 @@
 
 
 def edge_body(
-    flag, own_odd, own_even, odd, even, outer, sent_in, sent, change, old_change, halo, added_rows
+    flag, own_odd, own_even, odd, even, outer, sent_in, sent, change, old_change, added_rows
 ):
     space = lax.axis_index("space")
     turn = lax.axis_index("tm")
 
-    def take(low, high, own_low, own_high):
-        for side, (got, own) in enumerate(((low, own_low), (high, own_high))):
-            for k in range(3):
-                halo[side, k] = got[k]
-            halo[side, 3] = own[0]
-            halo[side, 4] = own[2]
-
-    pl.when(space % 2 == 0)(lambda: take(odd, even, own_odd, own_even))
-    pl.when(space % 2 == 1)(lambda: take(even, odd, own_even, own_odd))
-
-    flagged = flag[pl.ds(0, 1), pl.ds(0, 1)]
-    weight = jnp.where(turn > 0, 1.0, 0.0)
-    plane = iota((Z, Y), 0)
-
-    def beside(value):
-        total = jnp.where(plane == 0, 0.0, pltpu.roll(value, 1, 0))
-        total += jnp.where(plane == Z - 1, 0.0, pltpu.roll(value, Z - 1, 0))
-        return total + beside_lanes(value)
-
-    sums = [None] * 4
-    for side, inside in ((0, space > 0), (1, space < S - 1)):
-        keep = jnp.where(inside, 1.0, 0.0)
-        near, far, mob = keep * halo[side, 0], keep * halo[side, 1], halo[side, 2]
-        own, own_mob = halo[side, 3], halo[side, 4]
-        beyond = keep * fine_rule(near, far + own + beside(near), mob)
-        added = DIFFUSE * near
-        before = outer[side]
-        after = before + added
-        grown = after * (1.0 - after * after) - before * (1.0 - before * before)
-        first = added + DIFFUSE * (beyond + beside(added) - 6.0 * added)
-        first = flagged * (first + REACTION * own_mob * grown)
-        second = flagged * DIFFUSE * added
-        change[side, 0] = first
-        change[side, 1] = second
-        sums[side] = near + far
-        sums[2 + side] = first + second
-    halved = halve_lanes(jnp.concatenate(sums, axis=0))
-    for side in range(2):
-        coarse_side = (0.5 * DIFFUSE * 0.25) * halved[side * Z : (side + 1) * Z]
-        fine_side = 0.25 * halved[(2 + side) * Z : (3 + side) * Z]
-        old_change[side] = coarse_side
-        for tile, value in enumerate(edge_windows(fine_side - weight * coarse_side)):
-            added_rows[side, tile] = value
-    row = iota((CX, 128), 0)
-    for tile in range(T):
-        for z in range(HALF):
-            low = added_rows[0, tile, pl.ds(z, 1), :]
-            high = added_rows[1, tile, pl.ds(z, 1), :]
-            change_here = jnp.where(row == 0, low, jnp.where(row == CX - 1, high, 0.0))
-            sent[tile, z] = sent_in[tile, z] + change_here
+    def run(*sides):
+        flagged = flag[pl.ds(0, 1), pl.ds(0, 1)]
+        weight = jnp.where(turn > 0, 1.0, 0.0)
+        plane = iota((Z, Y), 0)
+
+        def beside(value):
+            total = jnp.where(plane == 0, 0.0, pltpu.roll(value, 1, 0))
+            total += jnp.where(plane == Z - 1, 0.0, pltpu.roll(value, Z - 1, 0))
+            return total + beside_lanes(value)
+
+        sums = [None] * 4
+        for side, inside in ((0, space > 0), (1, space < S - 1)):
+            keep = jnp.where(inside, 1.0, 0.0)
+            got, mine = sides[side]
+            near, far, mob = keep * got[0], keep * got[1], got[2]
+            own, own_mob = mine[0], mine[2]
+            beyond = keep * fine_rule(near, far + own + beside(near), mob)
+            added = DIFFUSE * near
+            before = outer[side]
+            after = before + added
+            grown = after * (1.0 - after * after) - before * (1.0 - before * before)
+            first = added + DIFFUSE * (beyond + beside(added) - 6.0 * added)
+            first = flagged * (first + REACTION * own_mob * grown)
+            second = flagged * DIFFUSE * added
+            change[side, 0] = first
+            change[side, 1] = second
+            sums[side] = near + far
+            sums[2 + side] = first + second
+        halved = halve_lanes(jnp.concatenate(sums, axis=0))
+        for side in range(2):
+            coarse_side = (0.5 * DIFFUSE * 0.25) * halved[side * Z : (side + 1) * Z]
+            fine_side = 0.25 * halved[(2 + side) * Z : (3 + side) * Z]
+            old_change[side] = coarse_side
+            for tile, value in enumerate(edge_windows(fine_side - weight * coarse_side)):
+                added_rows[side, tile] = value
+        row = iota((CX, 128), 0)
+        for tile in range(T):
+            for z in range(HALF):
+                low = added_rows[0, tile, pl.ds(z, 1), :]
+                high = added_rows[1, tile, pl.ds(z, 1), :]
+                change_here = jnp.where(row == 0, low, jnp.where(row == CX - 1, high, 0.0))
+                sent[tile, z] = sent_in[tile, z] + change_here
+
+    pl.when(space % 2 == 0)(lambda: run((odd, own_odd), (even, own_even)))
+    pl.when(space % 2 == 1)(lambda: run((even, own_even), (odd, own_odd)))
 
 
 def repair_body(fine_in, change, old_in, old_change, fine, coarse_old):
@@ -461,47 +456,61 @@
     return state
 
 
-def receive(odd, even, low, high):
+class Beside:
+    def __init__(self, ref, inside):
+        self.ref, self.keep = ref, jnp.where(inside, 1.0, 0.0)
+
+    def __getitem__(self, index):
+        return self.keep * self.ref[index]
+
+
+def sorted_by_side(run, *pairs):
     space = lax.axis_index("space")
 
-    def take(one, other):
-        low[...] = jnp.where(space > 0, one[...], 0.0)
-        high[...] = jnp.where(space < S - 1, other[...], 0.0)
-
-    pl.when(space % 2 == 0)(lambda: take(odd, even))
-    pl.when(space % 2 == 1)(lambda: take(even, odd))
+    def call_with(first):
+        sides = []
+        for pair in pairs:
+            low, high = pair[first], pair[1 - first]
+            sides.append((Beside(low, space > 0), Beside(high, space < S - 1)))
+        run(*sides)
+
+    pl.when(space % 2 == 0)(lambda: call_with(0))
+    pl.when(space % 2 == 1)(lambda: call_with(1))
 
 
 def chain_rate(below, mob_tile, above):
     return (2.0 * REACTION) * jnp.concatenate([below, mob_tile[...], above], axis=1)
 
 
-def chain_one_body(terms, mob_tile, odd, even, back, middle, low, high):
-    receive(odd, even, low, high)
-    extended = chain_parts(terms, [(EARLY, low, high)])
-    below, above = early_mobility(low, high)
-    rate = chain_rate(below, mob_tile, above)
+def chain_one_body(terms, mob_tile, odd, even, back, middle):
     weight = around_chain(lax.axis_index("space"), lax.axis_index("tm"))
     back[0] = jnp.zeros((4, CX, 128), jnp.float32)
-    state = run_chain(extended(0), extended, rate, weight, range(1, FIRST + 1), back)
-    middle[...] = state[:, CX : 2 * CX, :]
+
+    def run(early):
+        extended = chain_parts(terms, [(EARLY, *early)])
+        below, above = early_mobility(*early)
+        rate = chain_rate(below, mob_tile, above)
+        state = run_chain(extended(0), extended, rate, weight, range(1, FIRST + 1), back)
+        middle[...] = state[:, CX : 2 * CX, :]
+
+    sorted_by_side(run, (odd, even))
 
 
 def chain_two_body(
-    terms, mob_tile, odd, even, late_odd, late_even, first, middle, mid_odd, mid_even,
-    back, low, high, late_low, late_high, below, above,
+    terms, mob_tile, odd, even, late_odd, late_even, first, middle, mid_odd, mid_even, back
 ):
-    receive(odd, even, low, high)
-    receive(late_odd, late_even, late_low, late_high)
-    receive(mid_odd, mid_even, below, above)
-    late = LATE + (((LAST, 4), (MOBILITY, 4)),)
-    extended = chain_parts(terms, [(EARLY, low, high), (late, late_low, late_high)])
-    mob_below, mob_above = late_mobility(low, high, late_low, late_high)
-    rate = chain_rate(mob_below, mob_tile, mob_above)
     weight = around_chain(lax.axis_index("space"), lax.axis_index("tm"))
     back[pl.ds(0, FIRST + 1)] = first[...]
-    state = jnp.concatenate([below[...], middle[...], above[...]], axis=1)
-    run_chain(state, extended, rate, weight, range(FIRST + 1, T), back)
+    late_pairs = LATE + (((LAST, 4), (MOBILITY, 4)),)
+
+    def run(early, late, ends):
+        extended = chain_parts(terms, [(EARLY, *early), (late_pairs, *late)])
+        mob_below, mob_above = late_mobility(*early, *late)
+        rate = chain_rate(mob_below, mob_tile, mob_above)
+        state = jnp.concatenate([ends[0][...], middle[...], ends[1][...]], axis=1)
+        run_chain(state, extended, rate, weight, range(FIRST + 1, T), back)
+
+    sorted_by_side(run, (odd, even), (late_odd, late_even), (mid_odd, mid_even))
 
 
 def finish_body(fine, coarse_old, arrived, out_far, parts, out, done):
@@ -603,7 +612,7 @@
     sent, change, old_change = call(
         edge_body,
         [(T,) + tile, (2, 2, Z, Y), (2, Z, CY)],
-        [(2, 5, Z, Y), (2, T, HALF, 128)],
+        [(2, T, HALF, 128)],
     )(flag, own_odd, own_even, odd, even, outer, sent)
     terms = lax.all_to_all(sent, "tm", 0, 0)
     odd, even, late_odd, late_even = call(pack_chain_body, [early, early, late, late])(
@@ -616,11 +625,11 @@
     )
     odd, even, fine, coarse_old = lax.optimization_barrier((odd, even, fine, coarse_old))
     part = (4, CX, 128)
-    first, middle = call(chain_one_body, [(FIRST + 1,) + part, tile], [early, early])(
+    first, middle = call(chain_one_body, [(FIRST + 1,) + part, tile])(
         terms, mob_tile, odd, even
     )
     mid_odd, mid_even = exchange(middle, middle)
-    (back,) = call(chain_two_body, [(T,) + part], [early, early, late, late, tile, tile])(
+    (back,) = call(chain_two_body, [(T,) + part])(
         terms, mob_tile, odd, even, late_odd, late_even, first, middle, mid_odd, mid_even
     )
     arrived = lax.all_to_all(back, "tm", 0, 0)

time: 52.3 us -> 52.1 us (level)
  Pallas kernels: 8.56 us -> 7.73 us
    pallas_call x1, Pallas kernels: 1.52 us -> 0.8 us  [local(): call(second_body, [(ROWS, Y), (T,) + tile], [(Y // 256, ROWS, 128)])]
    all_to_all x1, blocking collectives: 16.7 us -> 17.2 us  [local(): terms = lax.all_to_all(sent, 'tm', 0, 0)]
  transfers between devices with their start and end apart: 8 -> 8, of which waited for: 2 -> 3; matrix products, arithmetic and copies ran while one was open for 0% -> 0% of each run, Pallas kernels for 8% -> 7%
where the time goes in v3:
time: 52.1 us; the launch traced here: 51.9 us
  blocking collectives  29.3 us (56%)
  starting transfers between devices  10.9 us (21%)
  Pallas kernels  7.73 us (15%)
  waiting for transfers between devices  3.23 us (6%)
  local copies, waits for them, and re-layouts  0.66 us (1%)
    all_to_all x1, blocking collectives, local(): terms = lax.all_to_all(sent, 'tm', 0, 0)  17.2 us
    all_to_all x1, blocking collectives, local(): arrived = lax.all_to_all(back, 'tm', 0, 0)  12.1 us
    ppermute x4, starting transfers between devices, exchange(): lax.ppermute(odd, ('tm', 'space'), route)  10.9 us
    ppermute x4, waiting for transfers between devices, exchange(): lax.ppermute(odd, ('tm', 'space'), route)  3.22 us
    pallas_call x1, Pallas kernels, local(): call(before_body, [(ROWS, Y), (CROWS, CY), tile, (2, Z, Y), (8, 128)], [(...  1.65 us
    pallas_call x1, Pallas kernels, finish(): pl.pallas_call(finish_body, out_shape=jax.ShapeDtypeStruct((ROWS, Y), jnp...  1.3 us
    pallas_call x1, Pallas kernels, pack_fine(): pl.pallas_call(pack_fine_body, out_shape=[rows, rows], in_specs=[pl.Block...  1.26 us
  transfers between devices with their start and end apart: 8, of which 3 were waited for; matrix products, arithmetic and copies ran while one was open for 0% of the time, Pallas kernels for 7%

profile of v3, /device:TPU:97, one launch (start us, length us, event | category | flops | bytes accessed | tf_op | source)
XLA Modules:
  0.0 51.9 jit_solution(4279052593202975249)
XLA Ops:
  0.0 0.0 copy-start
  0.0 0.0 copy-start.1
  0.0 1.3 %shard_map.47 = (f32[3,16,1024]{2,1,0:T(8,128)S(1)}, f32[3,16,1024]{2,1,0:T(8,128)S(1)}) custom-call(f32[16,16,1024]{2,1,0:T(8,128)} %bitcast.8, f32[16,16,1024]{2,1,0:T(8,128)} %mobility.1), custom_call_target="tpu_custom_call" | custom-call | bytes 400000 | tf_op jit(solution)/shard_map/pallas_call | solution.py:559
  1.3 3.5 %collective-permute-start = (f32[3,16,1024]{2,1,0:T(8,128)S(1)}, f32[3,16,1024]{2,1,0:T(8,128)S(1)}, u32[]{:S(2)}, u32[]{:S(2)}) collective-permute-start(f32[3,16,1024]{2,1,0:T(8,128)S(1)} %get-tuple-element.30.own_odd), channel_id=1, source_target_pairs={{0,16},{1,2},{2,1},{3,4},{4,3},{5,6},{6,5},{7,8},{8,7},{9,10},{10,... | collective-permute-start | bytes 589832 | tf_op jit(solution)/shard_map/ppermute | solution.py:596
  4.8 0.0 collective-permute-start.1
  4.8 0.0 copy-start.3
  4.8 0.0 copy-done
  4.8 0.0 copy-done.1
  4.8 0.6 %copy-done.3 = s32[16]{0:T(128)S(1)} copy-done((s32[16]{0:T(128)S(1)}, s32[16]{0:T(128)}, u32[]{:S(2)}) %copy-start.3) | copy-done | bytes 88
  5.4 0.0 copy-start.2
  5.4 1.7 %shard_map.46 = (f32[256,1024]{1,0:T(8,128)S(1)}, f32[128,512]{1,0:T(8,128)S(1)}, f32[8,8,128]{2,1,0:T(8,128)S(1)}, f32[2,16,1024]{2,1,0:T(8,128)S(1)}, f32[8,128]{1,0:T(8,128)S(1)}) custom-call(s32[1,16]{1,0:T(1,128)S(1)} %bitcast.11, f32[256,1024]{1,0:T(8,128)S(1)} %bitcast.9, f32[256,1024]{1,0:T(8,128)S(1)} %bitcast.6), custom_call_target="tpu_custom_call" | custom-call | bytes 4000000 | tf_op jit(solution)/shard_map/pallas_call | solution.py:606
  7.1 0.0 copy-done.2
  7.1 0.8 %shard_map.48 = (f32[256,1024]{1,0:T(8,128)S(1)}, f32[16,8,8,128]{3,2,1,0:T(8,128)S(1)}) custom-call(f32[8,128]{1,0:T(8,128)S(1)} %get-tuple-element.29.flag, f32[256,1024]{1,0:T(8,128)S(1)} %get-tuple-element.33.stepped, f32[256,1024]{1,0:T(8,128)S(1)} %bitcast.7, f32[128,512]{1,0:T(8,128)S(1)} %get-tuple-element.34.coarse_old.old_in, f32[256,1024]{1,0:T(8,128)S(1)} %bitcast.10), custom_call_target="tpu_custom_call" | custom-call | bytes 4000000 | tf_op jit(solution)/shard_map/pallas_call | solution.py:609
  7.9 0.2 collective-permute-done.odd
  8.1 0.0 collective-permute-done.1.even
  8.1 0.6 %shard_map.49 = (f32[16,8,8,128]{3,2,1,0:T(8,128)S(1)}, f32[2,2,16,1024]{3,2,1,0:T(8,128)S(1)}, f32[2,16,512]{2,1,0:T(8,128)S(1)}) custom-call(f32[8,128]{1,0:T(8,128)S(1)} %get-tuple-element.29.flag, f32[3,16,1024]{2,1,0:T(8,128)S(1)} %get-tuple-element.30.own_odd, f32[3,16,1024]{2,1,0:T(8,128)S(1)} %get-tuple-element.31.own_even, ...), custom_call_target="tpu_custom_call" | custom-call | bytes 4000000 | tf_op jit(solution)/shard_map/pallas_call | solution.py:612
  8.7 17.2 %all_to_all.10.terms = f32[16,8,8,128]{3,2,1,0:T(8,128)S(1)} all-to-all(f32[16,8,8,128]{3,2,1,0:T(8,128)S(1)} %get-tuple-element.36), channel_id=1, replica_groups=mesh['tm'=16,'space'=16] {'tm'}, dimensions={0} | all-to-all | bytes 1048576 | tf_op jit(solution)/shard_map/all_to_all | solution.py:617
  25.9 0.1 shard_map.50
  26.0 3.3 %collective-permute-start.2 = (f32[34,8,128]{2,1,0:T(8,128)S(1)}, f32[34,8,128]{2,1,0:T(8,128)S(1)}, u32[]{:S(2)}, u32[]{:S(2)}) collective-permute-start(f32[34,8,128]{2,1,0:T(8,128)S(1)} %get-tuple-element.38), channel_id=1, source_target_pairs={{0,16},{1,2},{2,1},{3,4},{4,3},{5,6},{6,5},{7,8},{8,7},{9,10},{10,... | collective-permute-start | bytes 417800 | tf_op jit(solution)/shard_map/ppermute | solution.py:596
  29.3 0.0 collective-permute-start.3
  29.3 1.1 %collective-permute-start.4 = (f32[32,8,128]{2,1,0:T(8,128)S(1)}, f32[32,8,128]{2,1,0:T(8,128)S(1)}, u32[]{:S(2)}, u32[]{:S(2)}) collective-permute-start(f32[32,8,128]{2,1,0:T(8,128)S(1)} %get-tuple-element.49), channel_id=1, source_target_pairs={{0,16},{1,2},{2,1},{3,4},{4,3},{5,6},{6,5},{7,8},{8,7},{9,10},{10,... | collective-permute-start | bytes 393224 | tf_op jit(solution)/shard_map/ppermute | solution.py:596
  30.4 0.0 collective-permute-start.5
  30.4 0.3 shard_map.51
  30.6 1.4 %collective-permute-done.2.odd = f32[34,8,128]{2,1,0:T(8,128)S(1)} collective-permute-done((f32[34,8,128]{2,1,0:T(8,128)S(1)}, f32[34,8,128]{2,1,0:T(8,128)S(1)}, u32[]{:S(2)}, u32[]{:S(2)}) %collective-permute-start.2) | collective-permute-done | bytes 139296 | tf_op jit(solution)/shard_map/ppermute | solution.py:596
  32.0 0.0 collective-permute-done.3.even
  32.1 0.9 %shard_map.52 = (f32[8,4,8,128]{3,2,1,0:T(8,128)S(1)}, f32[8,8,128]{2,1,0:T(8,128)S(1)}) custom-call(f32[16,8,8,128]{3,2,1,0:T(8,128)S(1)} %all_to_all.10.terms, f32[8,8,128]{2,1,0:T(8,128)S(1)} %get-tuple-element.37.mob_tile, f32[34,8,128]{2,1,0:T(8,128)S(1)} %collective-permute-done.2.odd, f32[34,8,128]{2,1,0:T(8,128)S(1)} %collective-permute-done.3.even), custom_call_target="tpu_custom_call" | custom-call | bytes 4000000 | tf_op jit(solution)/shard_map/pallas_call | solution.py:628
  32.9 3.0 %collective-permute-start.6 = (f32[8,8,128]{2,1,0:T(8,128)S(1)}, f32[8,8,128]{2,1,0:T(8,128)S(1)}, u32[]{:S(2)}, u32[]{:S(2)}) collective-permute-start(f32[8,8,128]{2,1,0:T(8,128)S(1)} %get-tuple-element.52.middle), channel_id=1, source_target_pairs={{0,16},{1,2},{2,1},{3,4},{4,3},{5,6},{6,5},{7,8},{8,7},{9,10},{10,... | collective-permute-start | bytes 98312 | tf_op jit(solution)/shard_map/ppermute | solution.py:596
  35.9 0.0 collective-permute-start.7
  35.9 0.0 collective-permute-done.4.late_odd
  36.0 0.0 collective-permute-done.5.late_even
  36.0 1.6 %collective-permute-done.6.mid_odd = f32[8,8,128]{2,1,0:T(8,128)S(1)} collective-permute-done((f32[8,8,128]{2,1,0:T(8,128)S(1)}, f32[8,8,128]{2,1,0:T(8,128)S(1)}, u32[]{:S(2)}, u32[]{:S(2)}) %collective-permute-start.6) | collective-permute-done | bytes 32800 | tf_op jit(solution)/shard_map/ppermute | solution.py:596
  37.5 0.0 collective-permute-done.7.mid_even
  37.5 1.0 %shard_map.53 = f32[16,4,8,128]{3,2,1,0:T(8,128)S(1)} custom-call(f32[16,8,8,128]{3,2,1,0:T(8,128)S(1)} %all_to_all.10.terms, f32[8,8,128]{2,1,0:T(8,128)S(1)} %get-tuple-element.37.mob_tile, f32[34,8,128]{2,1,0:T(8,128)S(1)} %collective-permute-done.2.odd, f32[34,8,128]{2,1,0:T(8,128)S(1)} %collective-permute-done.3.even, ...), custom_call_target="tpu_custom_call" | custom-call | bytes 4000000 | tf_op jit(solution)/shard_map/pallas_call | solution.py:632
  38.5 12.1 %all_to_all.11.arrived = f32[16,4,8,128]{3,2,1,0:T(8,128)S(1)} all-to-all(f32[16,4,8,128]{3,2,1,0:T(8,128)S(1)} %shard_map.53), channel_id=1, replica_groups=mesh['tm'=16,'space'=16] {'tm'}, dimensions={0} | all-to-all | bytes 524288 | tf_op jit(solution)/shard_map/all_to_all | solution.py:635
  50.6 1.3 %shard_map.54 = f32[256,1024]{1,0:T(8,128)} custom-call(f32[256,1024]{1,0:T(8,128)S(1)} %get-tuple-element.45.fine, f32[128,512]{1,0:T(8,128)S(1)} %get-tuple-element.46.coarse_old, f32[16,4,8,128]{3,2,1,0:T(8,128)S(1)} %all_to_all.11.arrived), custom_call_target="tpu_custom_call" | custom-call | bytes 4000000 | tf_op jit(solution)/shard_map/pallas_call | solution.py:571
Async XLA Ops:
  0.0 4.8 %copy-start = (f32[16,16,1024]{2,1,0:T(8,128)S(1)}, f32[16,16,1024]{2,1,0:T(8,128)}, u32[]{:S(2)}) copy-start(f32[16,16,1024]{2,1,0:T(8,128)} %mobility.1) | copy-start | bytes 3145732
  0.0 4.8 %copy-start.1 = (f32[1,16,16,1024]{3,2,1,0:T(8,128)S(1)}, f32[1,16,16,1024]{3,2,1,0:T(8,128)}, u32[]{:S(2)}) copy-start(f32[1,16,16,1024]{3,2,1,0:T(8,128)} %param.4) | copy-start | bytes 3145732
  1.3 6.9 %collective-permute-start = (f32[3,16,1024]{2,1,0:T(8,128)S(1)}, f32[3,16,1024]{2,1,0:T(8,128)S(1)}, u32[]{:S(2)}, u32[]{:S(2)}) collective-permute-start(f32[3,16,1024]{2,1,0:T(8,128)S(1)} %get-tuple-element.30.own_odd), channel_id=1, source_target_pairs={{0,16},{1,2},{2,1},{3,4},{4,3},{5,6},{6,5},{7,8},{8,7},{9,10},{10,... | collective-permute-start | bytes 589832 | tf_op jit(solution)/shard_map/ppermute | solution.py:596
  4.8 3.4 %collective-permute-start.1 = (f32[3,16,1024]{2,1,0:T(8,128)S(1)}, f32[3,16,1024]{2,1,0:T(8,128)S(1)}, u32[]{:S(2)}, u32[]{:S(2)}) collective-permute-start(f32[3,16,1024]{2,1,0:T(8,128)S(1)} %get-tuple-element.31.own_even), channel_id=1, source_target_pairs={{0,1},{1,0},{2,3},{3,2},{4,5},{5,4},{6,7},{7,6},{8,9},{9,8},{10,11... | collective-permute-start | bytes 589832 | tf_op jit(solution)/shard_map/ppermute | solution.py:596
  4.8 0.7 %copy-start.3 = (s32[16]{0:T(128)S(1)}, s32[16]{0:T(128)}, u32[]{:S(2)}) copy-start(s32[16]{0:T(128)} %param.7) | copy-start | bytes 196
  5.4 1.7 %copy-start.2 = (f32[1,16,16,1024]{3,2,1,0:T(8,128)S(1)}, f32[1,16,16,1024]{3,2,1,0:T(8,128)}, u32[]{:S(2)}) copy-start(f32[1,16,16,1024]{3,2,1,0:T(8,128)} %param.5) | copy-start | bytes 3145732
  26.0 6.1 %collective-permute-start.2 = (f32[34,8,128]{2,1,0:T(8,128)S(1)}, f32[34,8,128]{2,1,0:T(8,128)S(1)}, u32[]{:S(2)}, u32[]{:S(2)}) collective-permute-start(f32[34,8,128]{2,1,0:T(8,128)S(1)} %get-tuple-element.38), channel_id=1, source_target_pairs={{0,16},{1,2},{2,1},{3,4},{4,3},{5,6},{6,5},{7,8},{8,7},{9,10},{10,... | collective-permute-start | bytes 417800 | tf_op jit(solution)/shard_map/ppermute | solution.py:596
  29.3 2.7 %collective-permute-start.3 = (f32[34,8,128]{2,1,0:T(8,128)S(1)}, f32[34,8,128]{2,1,0:T(8,128)S(1)}, u32[]{:S(2)}, u32[]{:S(2)}) collective-permute-start(f32[34,8,128]{2,1,0:T(8,128)S(1)} %get-tuple-element.39), channel_id=1, source_target_pairs={{0,1},{1,0},{2,3},{3,2},{4,5},{5,4},{6,7},{7,6},{8,9},{9,8},{10,11... | collective-permute-start | bytes 417800 | tf_op jit(solution)/shard_map/ppermute | solution.py:596
  29.3 6.6 %collective-permute-start.4 = (f32[32,8,128]{2,1,0:T(8,128)S(1)}, f32[32,8,128]{2,1,0:T(8,128)S(1)}, u32[]{:S(2)}, u32[]{:S(2)}) collective-permute-start(f32[32,8,128]{2,1,0:T(8,128)S(1)} %get-tuple-element.49), channel_id=1, source_target_pairs={{0,16},{1,2},{2,1},{3,4},{4,3},{5,6},{6,5},{7,8},{8,7},{9,10},{10,... | collective-permute-start | bytes 393224 | tf_op jit(solution)/shard_map/ppermute | solution.py:596
  30.4 5.6 %collective-permute-start.5 = (f32[32,8,128]{2,1,0:T(8,128)S(1)}, f32[32,8,128]{2,1,0:T(8,128)S(1)}, u32[]{:S(2)}, u32[]{:S(2)}) collective-permute-start(f32[32,8,128]{2,1,0:T(8,128)S(1)} %get-tuple-element.50), channel_id=1, source_target_pairs={{0,1},{1,0},{2,3},{3,2},{4,5},{5,4},{6,7},{7,6},{8,9},{9,8},{10,11... | collective-permute-start | bytes 393224 | tf_op jit(solution)/shard_map/ppermute | solution.py:596
  32.9 4.6 %collective-permute-start.6 = (f32[8,8,128]{2,1,0:T(8,128)S(1)}, f32[8,8,128]{2,1,0:T(8,128)S(1)}, u32[]{:S(2)}, u32[]{:S(2)}) collective-permute-start(f32[8,8,128]{2,1,0:T(8,128)S(1)} %get-tuple-element.52.middle), channel_id=1, source_target_pairs={{0,16},{1,2},{2,1},{3,4},{4,3},{5,6},{6,5},{7,8},{8,7},{9,10},{10,... | collective-permute-start | bytes 98312 | tf_op jit(solution)/shard_map/ppermute | solution.py:596
  35.9 1.6 %collective-permute-start.7 = (f32[8,8,128]{2,1,0:T(8,128)S(1)}, f32[8,8,128]{2,1,0:T(8,128)S(1)}, u32[]{:S(2)}, u32[]{:S(2)}) collective-permute-start(f32[8,8,128]{2,1,0:T(8,128)S(1)} %get-tuple-element.52.middle), channel_id=1, source_target_pairs={{0,1},{1,0},{2,3},{3,2},{4,5},{5,4},{6,7},{7,6},{8,9},{9,8},{10,11... | collective-permute-start | bytes 98312 | tf_op jit(solution)/shard_map/ppermute | solution.py:596

commit v4 on v3

--- a/solution.py
+++ b/solution.py
@@ -274,7 +274,7 @@
 
 
 def edge_body(
-    flag, own_odd, own_even, odd, even, outer, sent_in, sent, change, old_change, added_rows
+    flag, own_odd, own_even, even, odd, outer, sent_in, sent, change, old_change, added_rows
 ):
     space = lax.axis_index("space")
     turn = lax.axis_index("tm")
@@ -613,7 +613,7 @@
         edge_body,
         [(T,) + tile, (2, 2, Z, Y), (2, Z, CY)],
         [(2, T, HALF, 128)],
-    )(flag, own_odd, own_even, odd, even, outer, sent)
+    )(flag, own_odd, own_even, even, odd, outer, sent)
     terms = lax.all_to_all(sent, "tm", 0, 0)
     odd, even, late_odd, late_even = call(pack_chain_body, [early, early, late, late])(
         terms, mob_tile

time: 52.1 us -> 52.4 us (level)
  Pallas kernels: 7.73 us -> 8.47 us
  starting transfers between devices: 10.9 us -> 10.3 us
    ppermute x4, starting transfers between devices: 10.9 us -> 9.53 us  [exchange(): lax.ppermute(odd, ('tm', 'space'), route)]
    ppermute x4, starting transfers between devices: 0.01 us -> 0.77 us  [exchange(): lax.ppermute(even, 'space', even_route)]
    pallas_call x1, Pallas kernels: 0.8 us -> 1.52 us  [local(): call(second_body, [(ROWS, Y), (T,) + tile], [(Y // 256, ROWS, 128)])]
    all_to_all x1, blocking collectives: 12.1 us -> 11.5 us  [local(): arrived = lax.all_to_all(back, 'tm', 0, 0)]
  transfers between devices with their start and end apart: 8 -> 8, of which waited for: 3 -> 2; matrix products, arithmetic and copies ran while one was open for 0% -> 0% of each run, Pallas kernels for 7% -> 8%
where the time goes in v4:
time: 52.4 us; the launch traced here: 52 us
  blocking collectives  29.1 us (56%)
  starting transfers between devices  10.3 us (20%)
  Pallas kernels  8.47 us (16%)
  waiting for transfers between devices  3.44 us (7%)
  local copies, waits for them, and re-layouts  0.66 us (1%)
    all_to_all x1, blocking collectives, local(): terms = lax.all_to_all(sent, 'tm', 0, 0)  17.6 us
    all_to_all x1, blocking collectives, local(): arrived = lax.all_to_all(back, 'tm', 0, 0)  11.5 us
    ppermute x4, starting transfers between devices, exchange(): lax.ppermute(odd, ('tm', 'space'), route)  9.53 us
    ppermute x4, waiting for transfers between devices, exchange(): lax.ppermute(odd, ('tm', 'space'), route)  3.43 us
    pallas_call x1, Pallas kernels, local(): call(before_body, [(ROWS, Y), (CROWS, CY), tile, (2, Z, Y), (8, 128)], [(...  1.65 us
    pallas_call x1, Pallas kernels, local(): call(second_body, [(ROWS, Y), (T,) + tile], [(Y // 256, ROWS, 128)])  1.52 us
    pallas_call x1, Pallas kernels, finish(): pl.pallas_call(finish_body, out_shape=jax.ShapeDtypeStruct((ROWS, Y), jnp...  1.3 us
    pallas_call x1, Pallas kernels, pack_fine(): pl.pallas_call(pack_fine_body, out_shape=[rows, rows], in_specs=[pl.Block...  1.26 us
  transfers between devices with their start and end apart: 8, of which 2 were waited for; matrix products, arithmetic and copies ran while one was open for 0% of the time, Pallas kernels for 8%

profile of v4, /device:TPU:97, one launch (start us, length us, event | category | flops | bytes accessed | tf_op | source)
XLA Modules:
  0.0 52.0 jit_solution(7809100326708312965)
XLA Ops:
  0.0 0.0 copy-start
  0.0 0.0 copy-start.1
  0.0 1.3 %shard_map.47 = (f32[3,16,1024]{2,1,0:T(8,128)S(1)}, f32[3,16,1024]{2,1,0:T(8,128)S(1)}) custom-call(f32[16,16,1024]{2,1,0:T(8,128)} %bitcast.8, f32[16,16,1024]{2,1,0:T(8,128)} %mobility.1), custom_call_target="tpu_custom_call" | custom-call | bytes 400000 | tf_op jit(solution)/shard_map/pallas_call | solution.py:559
  1.3 0.8 %collective-permute-start = (f32[3,16,1024]{2,1,0:T(8,128)S(1)}, f32[3,16,1024]{2,1,0:T(8,128)S(1)}, u32[]{:S(2)}, u32[]{:S(2)}) collective-permute-start(f32[3,16,1024]{2,1,0:T(8,128)S(1)} %get-tuple-element.31.own_even), channel_id=1, source_target_pairs={{0,1},{1,0},{2,3},{3,2},{4,5},{5,4},{6,7},{7,6},{8,9},{9,8},{10,11... | collective-permute-start | bytes 589832 | tf_op jit(solution)/shard_map/ppermute | solution.py:596
  2.0 2.8 %collective-permute-start.1 = (f32[3,16,1024]{2,1,0:T(8,128)S(1)}, f32[3,16,1024]{2,1,0:T(8,128)S(1)}, u32[]{:S(2)}, u32[]{:S(2)}) collective-permute-start(f32[3,16,1024]{2,1,0:T(8,128)S(1)} %get-tuple-element.30.own_odd), channel_id=1, source_target_pairs={{0,16},{1,2},{2,1},{3,4},{4,3},{5,6},{6,5},{7,8},{8,7},{9,10},{10,... | collective-permute-start | bytes 589832 | tf_op jit(solution)/shard_map/ppermute | solution.py:596
  4.9 0.0 copy-start.3
  4.9 0.0 copy-done
  4.9 0.0 copy-done.1
  4.9 0.6 %copy-done.3 = s32[16]{0:T(128)S(1)} copy-done((s32[16]{0:T(128)S(1)}, s32[16]{0:T(128)}, u32[]{:S(2)}) %copy-start.3) | copy-done | bytes 88
  5.5 0.0 copy-start.2
  5.5 1.6 %shard_map.46 = (f32[256,1024]{1,0:T(8,128)S(1)}, f32[128,512]{1,0:T(8,128)S(1)}, f32[8,8,128]{2,1,0:T(8,128)S(1)}, f32[2,16,1024]{2,1,0:T(8,128)S(1)}, f32[8,128]{1,0:T(8,128)S(1)}) custom-call(s32[1,16]{1,0:T(1,128)S(1)} %bitcast.11, f32[256,1024]{1,0:T(8,128)S(1)} %bitcast.9, f32[256,1024]{1,0:T(8,128)S(1)} %bitcast.6), custom_call_target="tpu_custom_call" | custom-call | bytes 4000000 | tf_op jit(solution)/shard_map/pallas_call | solution.py:606
  7.2 0.0 copy-done.2
  7.2 1.5 %shard_map.48 = (f32[256,1024]{1,0:T(8,128)S(1)}, f32[16,8,8,128]{3,2,1,0:T(8,128)S(1)}) custom-call(f32[8,128]{1,0:T(8,128)S(1)} %get-tuple-element.29.flag, f32[256,1024]{1,0:T(8,128)S(1)} %get-tuple-element.33.stepped, f32[256,1024]{1,0:T(8,128)S(1)} %bitcast.7, f32[128,512]{1,0:T(8,128)S(1)} %get-tuple-element.34.coarse_old.old_in, f32[256,1024]{1,0:T(8,128)S(1)} %bitcast.10), custom_call_target="tpu_custom_call" | custom-call | bytes 4000000 | tf_op jit(solution)/shard_map/pallas_call | solution.py:609
  8.7 0.0 collective-permute-done.even
  8.7 0.0 collective-permute-done.1.odd
  8.7 0.6 %shard_map.49 = (f32[16,8,8,128]{3,2,1,0:T(8,128)S(1)}, f32[2,2,16,1024]{3,2,1,0:T(8,128)S(1)}, f32[2,16,512]{2,1,0:T(8,128)S(1)}) custom-call(f32[8,128]{1,0:T(8,128)S(1)} %get-tuple-element.29.flag, f32[3,16,1024]{2,1,0:T(8,128)S(1)} %get-tuple-element.30.own_odd, f32[3,16,1024]{2,1,0:T(8,128)S(1)} %get-tuple-element.31.own_even, ...), custom_call_target="tpu_custom_call" | custom-call | bytes 4000000 | tf_op jit(solution)/shard_map/pallas_call | solution.py:612
  9.3 17.6 %all_to_all.10.terms = f32[16,8,8,128]{3,2,1,0:T(8,128)S(1)} all-to-all(f32[16,8,8,128]{3,2,1,0:T(8,128)S(1)} %get-tuple-element.36), channel_id=1, replica_groups=mesh['tm'=16,'space'=16] {'tm'}, dimensions={0} | all-to-all | bytes 1048576 | tf_op jit(solution)/shard_map/all_to_all | solution.py:617
  27.0 0.1 shard_map.50
  27.0 2.9 %collective-permute-start.2 = (f32[34,8,128]{2,1,0:T(8,128)S(1)}, f32[34,8,128]{2,1,0:T(8,128)S(1)}, u32[]{:S(2)}, u32[]{:S(2)}) collective-permute-start(f32[34,8,128]{2,1,0:T(8,128)S(1)} %get-tuple-element.38), channel_id=1, source_target_pairs={{0,16},{1,2},{2,1},{3,4},{4,3},{5,6},{6,5},{7,8},{8,7},{9,10},{10,... | collective-permute-start | bytes 417800 | tf_op jit(solution)/shard_map/ppermute | solution.py:596
  29.9 0.0 collective-permute-start.3
  29.9 0.9 %collective-permute-start.4 = (f32[32,8,128]{2,1,0:T(8,128)S(1)}, f32[32,8,128]{2,1,0:T(8,128)S(1)}, u32[]{:S(2)}, u32[]{:S(2)}) collective-permute-start(f32[32,8,128]{2,1,0:T(8,128)S(1)} %get-tuple-element.49), channel_id=1, source_target_pairs={{0,16},{1,2},{2,1},{3,4},{4,3},{5,6},{6,5},{7,8},{8,7},{9,10},{10,... | collective-permute-start | bytes 393224 | tf_op jit(solution)/shard_map/ppermute | solution.py:596
  30.8 0.0 collective-permute-start.5
  30.8 0.3 shard_map.51
  31.1 1.7 %collective-permute-done.2.odd = f32[34,8,128]{2,1,0:T(8,128)S(1)} collective-permute-done((f32[34,8,128]{2,1,0:T(8,128)S(1)}, f32[34,8,128]{2,1,0:T(8,128)S(1)}, u32[]{:S(2)}, u32[]{:S(2)}) %collective-permute-start.2) | collective-permute-done | bytes 139296 | tf_op jit(solution)/shard_map/ppermute | solution.py:596
  32.8 0.0 collective-permute-done.3.even
  32.8 0.9 %shard_map.52 = (f32[8,4,8,128]{3,2,1,0:T(8,128)S(1)}, f32[8,8,128]{2,1,0:T(8,128)S(1)}) custom-call(f32[16,8,8,128]{3,2,1,0:T(8,128)S(1)} %all_to_all.10.terms, f32[8,8,128]{2,1,0:T(8,128)S(1)} %get-tuple-element.37.mob_tile, f32[34,8,128]{2,1,0:T(8,128)S(1)} %collective-permute-done.2.odd, f32[34,8,128]{2,1,0:T(8,128)S(1)} %collective-permute-done.3.even), custom_call_target="tpu_custom_call" | custom-call | bytes 4000000 | tf_op jit(solution)/shard_map/pallas_call | solution.py:628
  33.7 2.9 %collective-permute-start.6 = (f32[8,8,128]{2,1,0:T(8,128)S(1)}, f32[8,8,128]{2,1,0:T(8,128)S(1)}, u32[]{:S(2)}, u32[]{:S(2)}) collective-permute-start(f32[8,8,128]{2,1,0:T(8,128)S(1)} %get-tuple-element.52.middle), channel_id=1, source_target_pairs={{0,16},{1,2},{2,1},{3,4},{4,3},{5,6},{6,5},{7,8},{8,7},{9,10},{10,... | collective-permute-start | bytes 98312 | tf_op jit(solution)/shard_map/ppermute | solution.py:596
  36.6 0.0 collective-permute-start.7
  36.6 0.0 collective-permute-done.4.late_odd
  36.6 0.0 collective-permute-done.5.late_even
  36.6 1.7 %collective-permute-done.6.mid_odd = f32[8,8,128]{2,1,0:T(8,128)S(1)} collective-permute-done((f32[8,8,128]{2,1,0:T(8,128)S(1)}, f32[8,8,128]{2,1,0:T(8,128)S(1)}, u32[]{:S(2)}, u32[]{:S(2)}) %collective-permute-start.6) | collective-permute-done | bytes 32800 | tf_op jit(solution)/shard_map/ppermute | solution.py:596
  38.3 0.0 collective-permute-done.7.mid_even
  38.3 1.0 %shard_map.53 = f32[16,4,8,128]{3,2,1,0:T(8,128)S(1)} custom-call(f32[16,8,8,128]{3,2,1,0:T(8,128)S(1)} %all_to_all.10.terms, f32[8,8,128]{2,1,0:T(8,128)S(1)} %get-tuple-element.37.mob_tile, f32[34,8,128]{2,1,0:T(8,128)S(1)} %collective-permute-done.2.odd, f32[34,8,128]{2,1,0:T(8,128)S(1)} %collective-permute-done.3.even, ...), custom_call_target="tpu_custom_call" | custom-call | bytes 4000000 | tf_op jit(solution)/shard_map/pallas_call | solution.py:632
  39.3 11.5 %all_to_all.11.arrived = f32[16,4,8,128]{3,2,1,0:T(8,128)S(1)} all-to-all(f32[16,4,8,128]{3,2,1,0:T(8,128)S(1)} %shard_map.53), channel_id=1, replica_groups=mesh['tm'=16,'space'=16] {'tm'}, dimensions={0} | all-to-all | bytes 524288 | tf_op jit(solution)/shard_map/all_to_all | solution.py:635
  50.7 1.3 %shard_map.54 = f32[256,1024]{1,0:T(8,128)} custom-call(f32[256,1024]{1,0:T(8,128)S(1)} %get-tuple-element.45.fine, f32[128,512]{1,0:T(8,128)S(1)} %get-tuple-element.46.coarse_old, f32[16,4,8,128]{3,2,1,0:T(8,128)S(1)} %all_to_all.11.arrived), custom_call_target="tpu_custom_call" | custom-call | bytes 4000000 | tf_op jit(solution)/shard_map/pallas_call | solution.py:571
Async XLA Ops:
  0.0 4.9 %copy-start = (f32[16,16,1024]{2,1,0:T(8,128)S(1)}, f32[16,16,1024]{2,1,0:T(8,128)}, u32[]{:S(2)}) copy-start(f32[16,16,1024]{2,1,0:T(8,128)} %mobility.1) | copy-start | bytes 3145732
  0.0 4.9 %copy-start.1 = (f32[1,16,16,1024]{3,2,1,0:T(8,128)S(1)}, f32[1,16,16,1024]{3,2,1,0:T(8,128)}, u32[]{:S(2)}) copy-start(f32[1,16,16,1024]{3,2,1,0:T(8,128)} %param.4) | copy-start | bytes 3145732
  1.3 7.5 %collective-permute-start = (f32[3,16,1024]{2,1,0:T(8,128)S(1)}, f32[3,16,1024]{2,1,0:T(8,128)S(1)}, u32[]{:S(2)}, u32[]{:S(2)}) collective-permute-start(f32[3,16,1024]{2,1,0:T(8,128)S(1)} %get-tuple-element.31.own_even), channel_id=1, source_target_pairs={{0,1},{1,0},{2,3},{3,2},{4,5},{5,4},{6,7},{7,6},{8,9},{9,8},{10,11... | collective-permute-start | bytes 589832 | tf_op jit(solution)/shard_map/ppermute | solution.py:596
  2.0 6.7 %collective-permute-start.1 = (f32[3,16,1024]{2,1,0:T(8,128)S(1)}, f32[3,16,1024]{2,1,0:T(8,128)S(1)}, u32[]{:S(2)}, u32[]{:S(2)}) collective-permute-start(f32[3,16,1024]{2,1,0:T(8,128)S(1)} %get-tuple-element.30.own_odd), channel_id=1, source_target_pairs={{0,16},{1,2},{2,1},{3,4},{4,3},{5,6},{6,5},{7,8},{8,7},{9,10},{10,... | collective-permute-start | bytes 589832 | tf_op jit(solution)/shard_map/ppermute | solution.py:596
  4.9 0.7 %copy-start.3 = (s32[16]{0:T(128)S(1)}, s32[16]{0:T(128)}, u32[]{:S(2)}) copy-start(s32[16]{0:T(128)} %param.7) | copy-start | bytes 196
  5.5 1.7 %copy-start.2 = (f32[1,16,16,1024]{3,2,1,0:T(8,128)S(1)}, f32[1,16,16,1024]{3,2,1,0:T(8,128)}, u32[]{:S(2)}) copy-start(f32[1,16,16,1024]{3,2,1,0:T(8,128)} %param.5) | copy-start | bytes 3145732
  27.0 5.8 %collective-permute-start.2 = (f32[34,8,128]{2,1,0:T(8,128)S(1)}, f32[34,8,128]{2,1,0:T(8,128)S(1)}, u32[]{:S(2)}, u32[]{:S(2)}) collective-permute-start(f32[34,8,128]{2,1,0:T(8,128)S(1)} %get-tuple-element.38), channel_id=1, source_target_pairs={{0,16},{1,2},{2,1},{3,4},{4,3},{5,6},{6,5},{7,8},{8,7},{9,10},{10,... | collective-permute-start | bytes 417800 | tf_op jit(solution)/shard_map/ppermute | solution.py:596
  29.9 2.9 %collective-permute-start.3 = (f32[34,8,128]{2,1,0:T(8,128)S(1)}, f32[34,8,128]{2,1,0:T(8,128)S(1)}, u32[]{:S(2)}, u32[]{:S(2)}) collective-permute-start(f32[34,8,128]{2,1,0:T(8,128)S(1)} %get-tuple-element.39), channel_id=1, source_target_pairs={{0,1},{1,0},{2,3},{3,2},{4,5},{5,4},{6,7},{7,6},{8,9},{9,8},{10,11... | collective-permute-start | bytes 417800 | tf_op jit(solution)/shard_map/ppermute | solution.py:596
  29.9 6.6 %collective-permute-start.4 = (f32[32,8,128]{2,1,0:T(8,128)S(1)}, f32[32,8,128]{2,1,0:T(8,128)S(1)}, u32[]{:S(2)}, u32[]{:S(2)}) collective-permute-start(f32[32,8,128]{2,1,0:T(8,128)S(1)} %get-tuple-element.49), channel_id=1, source_target_pairs={{0,16},{1,2},{2,1},{3,4},{4,3},{5,6},{6,5},{7,8},{8,7},{9,10},{10,... | collective-permute-start | bytes 393224 | tf_op jit(solution)/shard_map/ppermute | solution.py:596
  30.8 5.8 %collective-permute-start.5 = (f32[32,8,128]{2,1,0:T(8,128)S(1)}, f32[32,8,128]{2,1,0:T(8,128)S(1)}, u32[]{:S(2)}, u32[]{:S(2)}) collective-permute-start(f32[32,8,128]{2,1,0:T(8,128)S(1)} %get-tuple-element.50), channel_id=1, source_target_pairs={{0,1},{1,0},{2,3},{3,2},{4,5},{5,4},{6,7},{7,6},{8,9},{9,8},{10,11... | collective-permute-start | bytes 393224 | tf_op jit(solution)/shard_map/ppermute | solution.py:596
  33.7 4.6 %collective-permute-start.6 = (f32[8,8,128]{2,1,0:T(8,128)S(1)}, f32[8,8,128]{2,1,0:T(8,128)S(1)}, u32[]{:S(2)}, u32[]{:S(2)}) collective-permute-start(f32[8,8,128]{2,1,0:T(8,128)S(1)} %get-tuple-element.52.middle), channel_id=1, source_target_pairs={{0,16},{1,2},{2,1},{3,4},{4,3},{5,6},{6,5},{7,8},{8,7},{9,10},{10,... | collective-permute-start | bytes 98312 | tf_op jit(solution)/shard_map/ppermute | solution.py:596
  36.6 1.7 %collective-permute-start.7 = (f32[8,8,128]{2,1,0:T(8,128)S(1)}, f32[8,8,128]{2,1,0:T(8,128)S(1)}, u32[]{:S(2)}, u32[]{:S(2)}) collective-permute-start(f32[8,8,128]{2,1,0:T(8,128)S(1)} %get-tuple-element.52.middle), channel_id=1, source_target_pairs={{0,1},{1,0},{2,3},{3,2},{4,5},{5,4},{6,7},{7,6},{8,9},{9,8},{10,11... | collective-permute-start | bytes 98312 | tf_op jit(solution)/shard_map/ppermute | solution.py:596
